TPU v7x, 32 devices: a whole 2x2x4 slice. The times are simulated.
32 devices in a mesh: dp: 8 (over y, x, core), seq: 4 (over z).
Axes of the slice: x: 2, y: 2, z: 4, core: 2. Of those that a mesh axis runs over, the one named last changes fastest.
Arguments:
- inputs: bfloat16 [8, 2048, 1472], P('dp', 'seq'), may hold values from -6 to 6
- segments: int32 [8, 2048], P('dp', 'seq'), may hold values from 0 to 5, never falling along the last dimension, each value on 1 to 800 neighbouring positions
- cotangent: bfloat16 [8, 2048, 1472], P('dp', 'seq'), may hold values from -6 to 6
- w_query: bfloat16 [1472, 384], P('dp', 'seq'), may hold values from -0.0546875 to 0.0546875
- w_key: bfloat16 [1472, 384], P('dp', 'seq'), may hold values from -0.109375 to 0.109375
- w_value: bfloat16 [1472, 384], P('dp', 'seq'), may hold values from -0.15625 to 0.15625
- w_out: bfloat16 [384, 1472], P('seq', 'dp'), may hold values from -1.25 to 1.25
- w_gate: bfloat16 [1472, 3584], P('dp', 'seq'), may hold values from -0.15625 to 0.15625
- w_up: bfloat16 [1472, 3584], P('dp', 'seq'), may hold values from -0.15625 to 0.15625
- w_down: bfloat16 [3584, 1472], P('seq', 'dp'), may hold values from -0.1875 to 0.1875
- gain_attn: bfloat16 [1472], P('dp'), may hold values from 0.25 to 1.75
- gain_ffn: bfloat16 [1472], P('dp'), may hold values from 0.25 to 1.75
- rel_table: bfloat16 [32, 6], P('dp'), may hold values from -4 to 4
Outputs:
- outputs: bfloat16 [8, 2048, 1472], P('dp', 'seq')
- input_grad: bfloat16 [8, 2048, 1472], P('dp', 'seq')
- grad_query: float32 [1472, 384], P('dp', 'seq')
- grad_key: float32 [1472, 384], P('dp', 'seq')
- grad_value: float32 [1472, 384], P('dp', 'seq')
- grad_out: float32 [384, 1472], P('seq', 'dp')
- grad_gate: float32 [1472, 3584], P('dp', 'seq')
- grad_up: float32 [1472, 3584], P('dp', 'seq')
- grad_down: float32 [3584, 1472], P('seq', 'dp')
- grad_gain_attn: float32 [1472], P('dp')
- grad_gain_ffn: float32 [1472], P('dp')
- grad_table: float32 [32, 6], P('dp')
Inputs may be any that keep to these rules, and one draw needn't show every extreme that they name: `segments`: along each sequence the ids never fall; each id names one document of 1 to 800 tokens.
All inputs are finite; a program needn't handle non-finite values.
Results may differ from a plain program's by a relative error of at most 0.02.
Values may be sent and summed in bfloat16 or wider, within the bound.
No kernel may reach another device: no remote copies, remote signals or barrier semaphores. Data moves between devices by JAX's collectives and lax.ppermute only.
A program may use at most 256 MiB of HBM per device.

v0:
```python
import math
from functools import partial

import jax
import jax.numpy as jnp
import numpy as np
from jax import lax
from jax.experimental import pallas as pl
from jax.experimental.pallas import tpu as pltpu
from jax.sharding import PartitionSpec as P

HEADS = 6
BUCKETS = 32
MAX_DOC = 800
BLK = 256
SPAN = 1024
EPS = 1e-06
MASKED = -1e30
F32 = jnp.float32
BF16 = jnp.bfloat16
VMEM_CAP = 58 * 1024 * 1024
LANES = 128
GELU_K = math.sqrt(2.0 / math.pi)
GELU_A = 0.044715


def bucket_table():
    relative = np.arange(SPAN) - SPAN // 2
    distance = np.abs(relative)
    steps = np.array([12, 16, 23, 32, 46, 64, 91])
    levels = (distance[:, None] >= steps[None, :]).sum(axis=1)
    inside = np.where(distance < 8, distance, 8 + levels)
    return (inside + 16 * (relative > 0)).astype(np.int32)


class Moves:
    def __init__(self, n_dp, n_seq):
        self.n_dp, self.n_seq = n_dp, n_seq
        plane = n_dp // 2
        side = int(round(math.sqrt(plane)))
        self.size = {"a": plane // side, "b": side, "c": 2, "z": n_seq}
        dp = lax.axis_index("dp")
        self.last = {}
        self.index = {
            "a": dp // (2 * side),
            "b": (dp // 2) % side,
            "c": dp % 2,
            "z": lax.axis_index("seq"),
        }

    def rotate(self, x, axis):
        n = self.size[axis]
        if axis == "z":
            return lax.ppermute(x, "seq", [(i, (i + 1) % n) for i in range(n)])
        pairs = []
        side = self.size["b"]
        for i in range(self.n_dp):
            a, b, c = i // (2 * side), (i // 2) % side, i % 2
            if axis == "a":
                a = (a + 1) % n
            elif axis == "b":
                b = (b + 1) % n
            else:
                c = 1 - c
            pairs.append((i, (a * side + b) * 2 + c))
        return lax.ppermute(x, "dp", pairs)

    def zperm(self, x, pairs):
        return lax.ppermute(x, "seq", pairs)

    def same_core(self):
        return [list(range(c, self.n_dp, 2)) for c in range(2)]

    def ring(self, x, waits=()):
        parts = []
        for step in range(self.n_seq - 1):
            x = self.rotate(after(x, *waits[step]) if step < len(waits) else x, "z")
            parts.append(x)
        return parts

    def gather(self, x, axis, at=0):
        n, i = self.size[axis], self.index[axis]
        if n == 2:
            other = self.rotate(x, axis)
            return ordered(i == 0, x, other, at)
        parts = [x]
        for _ in range(n - 1):
            parts.append(self.rotate(parts[-1], axis))
        turned = jnp.stack(parts[::-1] + parts[::-1], 0)
        full = lax.dynamic_slice_in_dim(turned, n - 1 - i, n, 0)
        return jnp.moveaxis(full, 0, at)

    def scatter(self, x, axis, at=0, out=BF16):
        n, i = self.size[axis], self.index[axis]
        take = lambda k: lax.dynamic_index_in_dim(x, k, at, keepdims=False)
        if n == 2:
            other = self.rotate(take(1 - i), axis)
            return add(take(i), other, out)
        acc = take((i + n - 1) % n)
        for step in range(n - 1):
            got = self.rotate(acc, axis)
            last = step == n - 2
            acc = add(take((i + 2 * n - 2 - step) % n), got, out if last else BF16)
        return acc


def after(x, *others):
    others = [o for o in others if o is not None]
    return lax.optimization_barrier((x, *others))[0] if others else x


def add(x, y, out):
    return (x.astype(F32) + y.astype(F32)).astype(out)


def ordered(first, x, y, at):
    return jnp.stack([jnp.where(first, x, y), jnp.where(first, y, x)], at)


def z_gather(mv, w, waits=()):
    z, n = mv.index["z"], mv.n_seq
    blocks = [w] + mv.ring(w, waits)
    turned = jnp.stack(blocks[::-1] + blocks[::-1], 0)
    return lax.dynamic_slice_in_dim(turned, n - 1 - z, n, 0)


def small_plane(mv):
    return mv.size["a"] == 2 and mv.size["b"] == 2 and mv.n_seq == 4


def gather_core(mv, w, ready):
    k, rows, cols = w.shape
    c = mv.index["c"]
    full = lax.all_gather(w, "seq")
    zh = mv.n_seq // 2
    keep = lax.dynamic_slice_in_dim(full, c * zh, zh, 0)
    send = lax.dynamic_slice_in_dim(full, (1 - c) * zh, zh, 0)
    recv = mv.rotate(after(send, *ready), "c")
    block = ordered(c == 0, keep, recv, 2)
    return [block[j].reshape(k, 2 * rows, cols) for j in range(zh)]


def scatter_plane(mv, grad):
    quarter, k, rows, cols = grad.shape
    chips = mv.n_dp // 2
    x = grad
    if chips != quarter:
        x = jnp.moveaxis(grad, 1, 0).reshape(k, chips, quarter * rows // chips, cols)
        x = jnp.moveaxis(x, 0, 1)
    x = lax.psum_scatter(x, "dp", scatter_dimension=0, axis_index_groups=mv.same_core())
    x = x.reshape(k, 2, x.shape[1] // 2, cols)
    return x


def swap_cores(mv, x):
    c = mv.index["c"]
    take = lambda i: lax.dynamic_index_in_dim(x, i, 1, keepdims=False)
    return take(c), mv.rotate(take(1 - c), "c")


class ZSum:
    def __init__(self, mv, j, x):
        self.mv, self.j, self.x = mv, j, x

    def swap(self, wait):
        c = self.mv.index["c"]
        x = after(self.x, wait)
        take = lambda i: lax.dynamic_index_in_dim(x, i, 1, keepdims=False)
        mine, other = take(c), self.mv.rotate(take(1 - c), "c")
        here = (self.mv.index["z"] // 2) == c
        self.pair = mine, other
        self.near, self.far = jnp.where(here, mine, other), jnp.where(here, other, mine)
        return other

    def inwards(self, wait=None):
        got = self.mv.zperm(after(self.far, wait), [(0, 1), (3, 2)])
        self.far = add(self.far, got, BF16)
        return got

    def across(self, wait=None):
        got = self.mv.zperm(after(self.far, wait), [(1, 2), (2, 1)])
        self.near = add(self.near, got, BF16)
        return got

    def home(self, wait=None):
        j = self.j
        got = self.mv.zperm(after(self.near, wait), [(1 - j, j), (3 - j, 2 + j)])
        self.total = add(self.near, got, F32)
        return got


def z_totals(mv, sums):
    z, c = mv.index["z"], mv.index["c"]
    join = lambda parts: jnp.concatenate(parts, 0)
    if mv.n_seq == 4:
        first, second = (join([u.total for u in units]) for units in sums)
        return jnp.where(z % 2 == 0, first, second)
    full = jnp.stack(
        [ordered(c == 0, *(join([u.pair[i] for u in units]) for i in range(2)), 0) for units in sums], 1
    )
    return mv.scatter(full.reshape((mv.n_seq,) + full.shape[2:]), "z", 0, F32)


def gather_small(mv, w):
    full = z_gather(mv, w)
    half = mv.n_seq // 2
    lo_one = mv.gather(full[:half], "b", 1)
    hi_one = mv.gather(full[half:], "a", 1)
    lo = mv.gather(lo_one, "a", 1)
    hi = mv.gather(hi_one, "b", 2)
    both = jnp.concatenate([lo, hi], 0)
    both = mv.gather(both, "c", 3)
    return both.reshape((mv.n_seq, mv.n_dp) + w.shape), (full, (lo_one, hi_one), (lo, hi))


def scatter_small(mv, send, keep):
    both = add(keep, mv.rotate(send, "c"), BF16)
    x = lax.psum_scatter(both, "dp", scatter_dimension=0, axis_index_groups=mv.same_core())
    return lax.psum_scatter(x, "seq", scatter_dimension=0).astype(F32), both


def reach_of(rows, n_seq):
    need, parts = MAX_DOC - 1, []
    while need > 0 and len(parts) + 1 < n_seq:
        parts.append(min(rows, -(-need // LANES) * LANES))
        need -= rows
    return parts


def halo(mv, x, chained=True):
    rows, n = x.shape[1], mv.n_seq
    left, right = [], []
    own = x
    for hop, cols in enumerate(reach_of(rows, n)):
        step = hop + 1
        if chained and hop > 0:
            x = after(x, left[0], right[-1])
        left.insert(0, mv.zperm(x[:, rows - cols :], [(i, i + step) for i in range(n - step)]))
        right.append(mv.zperm(x[:, :cols], [(i + step, i) for i in range(n - step)]))
    return left + [own] + right


def dot(x, y, dims):
    return lax.dot_general(x, y, (dims, ((), ())), preferred_element_type=F32)


def nt(x, y):
    return dot(x, y, ((1,), (1,)))


def nn(x, y):
    return dot(x, y, ((1,), (0,)))


def tn(x, y):
    return dot(x, y, ((0,), (0,)))


def make_tiles(vec_ref, tiles):
    for h in range(HEADS):
        line = vec_ref[h : h + 1, :]
        wide = jnp.broadcast_to(line, (BLK, SPAN))
        rolled = pltpu.roll(wide, 0, 1, stride=1, stride_axis=0)
        tiles[h * 5] = jnp.broadcast_to(line[:, :1], (BLK, BLK))
        tiles[h * 5 + 4] = jnp.broadcast_to(line[:, SPAN - 1 :], (BLK, BLK))
        for d in (-1, 0, 1):
            at = SPAN // 2 + BLK * d
            tiles[h * 5 + 2 + d] = rolled[:, at : at + BLK]


def class_of(query_block, key_block):
    return jnp.clip(query_block - key_block, -2, 2) + 2


def lay_out(off, pieces, whole):
    middle = len(pieces) // 2
    at = off - sum(p.shape[1] for p in pieces[:middle])
    if at > 0:
        whole[:, :at] = jnp.zeros((whole.shape[0], at), whole.dtype)
    for p in pieces:
        whole[:, at : at + p.shape[1]] = p[...]
        at += p.shape[1]
    if at < whole.shape[1]:
        whole[:, at:] = jnp.zeros((whole.shape[0], whole.shape[1] - at), whole.dtype)


def block_at(k):
    return pl.ds(pl.multiple_of(k * BLK, BLK), BLK)


def forward_kernel(off, count, lohi, vec, q_ref, segq, segk, *rest):
    pieces = rest[:count]
    out, exact, lse, split, tiles, kv = rest[count:]
    i = pl.program_id(0)

    @pl.when(i == 0)
    def _():
        make_tiles(vec, tiles)
        lay_out(off, pieces, kv)

    own = off // BLK + i
    inner = HEADS * 64
    low, high = lohi[i, 0], lohi[i, 1]
    seg_row = segq[0]
    split[...] = jnp.zeros_like(split)
    lse[...] = jnp.zeros_like(lse)
    for pair in range(HEADS // 2):
        heads = (2 * pair, 2 * pair + 1)
        qs = [q_ref[h * 64 : h * 64 + 64, :] for h in heads]

        def body(kb, state):
            cols = block_at(kb)
            same = segk[cols, :] == seg_row
            kind = class_of(own, kb)
            new = []
            for e, h in enumerate(heads):
                peak, total, acc = state[e]
                s = tn(kv[h * 64 : h * 64 + 64, cols], qs[e]) + tiles[h * 5 + kind]
                s = jnp.where(same, s, MASKED)
                top = jnp.maximum(peak, jnp.max(s, axis=0, keepdims=True))
                fade = jnp.exp(peak - top)
                p = jnp.exp(s - top)
                total = total * fade + jnp.sum(p, axis=0, keepdims=True)
                acc = acc * fade + nn(kv[inner + h * 64 : inner + h * 64 + 64, cols], p.astype(BF16))
                new.append((top, total, acc))
            return tuple(new)

        start = (
            jnp.full((1, BLK), MASKED, F32),
            jnp.zeros((1, BLK), F32),
            jnp.zeros((64, BLK), F32),
        )
        state = lax.fori_loop(low, high, body, (start, start))
        for e, h in enumerate(heads):
            peak, total, acc = state[e]
            done = acc / total
            out[h * 64 : h * 64 + 64, :] = done.astype(BF16)
            exact[h * 64 : h * 64 + 64, :] = done
            log = peak + jnp.log(total)
            lse[h : h + 1, :] = log
            for part in range(3):
                piece = log.astype(BF16)
                split[part * 8 + h : part * 8 + h + 1, :] = piece
                log = log - piece.astype(F32)


def query_kernel(off, count, lohi, vec, q_ref, do_ref, lse, delta, segq, segk, *rest):
    pieces = rest[:count]
    dq, near, far, tiles, sums, kv = rest[count:]
    i = pl.program_id(0)

    @pl.when(i == 0)
    def _():
        make_tiles(vec, tiles)
        lay_out(off, pieces, kv)
        sums[...] = jnp.zeros_like(sums)

    own = off // BLK + i
    inner = HEADS * 64
    low, high = lohi[i, 0], lohi[i, 1]
    seg_row = segq[0]
    for pair in range(HEADS // 2):
        heads = (2 * pair, 2 * pair + 1)
        qs = [q_ref[h * 64 : h * 64 + 64, :] for h in heads]
        dos = [do_ref[h * 64 : h * 64 + 64, :] for h in heads]

        def body(kb, state):
            cols = block_at(kb)
            same = segk[cols, :] == seg_row
            kind = class_of(own, kb)
            new = []
            for e, h in enumerate(heads):
                keys = kv[h * 64 : h * 64 + 64, cols]
                s = tn(keys, qs[e]) + tiles[h * 5 + kind]
                s = jnp.where(same, s, MASKED)
                p = jnp.exp(s - lse[h : h + 1, :])
                dp = tn(kv[inner + h * 64 : inner + h * 64 + 64, cols], dos[e])
                ds = p * (dp - delta[h : h + 1, :])
                at = h * 5 + kind
                sums[at] = sums[at] + ds
                new.append(state[e] + nn(keys, ds.astype(BF16)))
            return tuple(new)

        start = jnp.zeros((64, BLK), F32)
        state = lax.fori_loop(low, high, body, (start, start))
        for e, h in enumerate(heads):
            dq[h * 64 : h * 64 + 64, :] = state[e].astype(BF16)

    @pl.when(i == pl.num_programs(0) - 1)
    def _():
        for h in range(HEADS):
            zero = jnp.zeros((BLK, BLK), F32)
            x = jnp.concatenate([sums[h * 5 + 1], sums[h * 5 + 2], sums[h * 5 + 3], zero], axis=1)
            n = BLK // 2
            while n >= 8:
                x = x[:n] + pltpu.roll(x[n:], SPAN - n, 1)
                n //= 2
            row = lax.broadcasted_iota(jnp.int32, x.shape, 0)
            for n in (4, 2, 1):
                x = jnp.where((row & n) != 0, pltpu.roll(x, SPAN - n, 1), x)
            near[h] = x
            far[h, 0] = jnp.sum(sums[h * 5].reshape(BLK // 8, 8, BLK), axis=0)
            far[h, 1] = jnp.sum(sums[h * 5 + 4].reshape(BLK // 8, 8, BLK), axis=0)


def key_kernel(off, count, lohi, vec, k_ref, v_ref, segq, segk, *rest):
    queries, answers = rest[:count], rest[count : 2 * count]
    dk, dv, tiles, qs, dos = rest[2 * count :]
    i = pl.program_id(0)

    @pl.when(i == 0)
    def _():
        make_tiles(vec, tiles)
        lay_out(off, queries, qs)
        lay_out(off, answers, dos)

    own = off // BLK + i
    inner = HEADS * 64
    low, high = lohi[i, 0], lohi[i, 1]
    seg_col = segk[...]
    for pair in range(HEADS // 2):
        heads = (2 * pair, 2 * pair + 1)
        ks = [k_ref[h * 64 : h * 64 + 64, :] for h in heads]
        vs = [v_ref[h * 64 : h * 64 + 64, :] for h in heads]

        def body(qb, state):
            cols = block_at(qb)
            same = seg_col == segq[qb]
            kind = class_of(qb, own)
            logs = qs[inner : inner + 8, cols].astype(F32)
            logs = logs + qs[inner + 8 : inner + 16, cols].astype(F32)
            logs = logs + qs[inner + 16 : inner + 24, cols].astype(F32)
            deltas = dos[inner : inner + 8, cols].astype(F32)
            deltas = deltas + dos[inner + 8 : inner + 16, cols].astype(F32)
            new = []
            for e, h in enumerate(heads):
                q, do = qs[h * 64 : h * 64 + 64, cols], dos[h * 64 : h * 64 + 64, cols]
                s = tn(ks[e], q) + tiles[h * 5 + kind]
                s = jnp.where(same, s, MASKED)
                p = jnp.exp(s - logs[h : h + 1, :])
                ds = p * (tn(vs[e], do) - deltas[h : h + 1, :])
                to_k, to_v = state[e]
                new.append((to_k + nt(q, ds.astype(BF16)), to_v + nt(do, p.astype(BF16))))
            return tuple(new)

        start = jnp.zeros((64, BLK), F32)
        state = lax.fori_loop(low, high, body, ((start, start), (start, start)))
        for e, h in enumerate(heads):
            dk[h * 64 : h * 64 + 64, :] = state[e][0].astype(BF16)
            dv[h * 64 : h * 64 + 64, :] = state[e][1].astype(BF16)


def whole_block(shape):
    return pl.BlockSpec(shape, lambda i: (0,) * len(shape))


def col_block(rows):
    return pl.BlockSpec((rows, BLK), lambda i: (0, i))


SMEM_SPEC = pl.BlockSpec(memory_space=pltpu.SMEM)
COL_SEGS = pl.BlockSpec((BLK, 1), lambda i: (i, 0))
ROW_SEGS = pl.BlockSpec((1, 1, BLK), lambda i: (i, 0, 0))
TILES = pltpu.VMEM((HEADS * 5, BLK, BLK), F32)
LIGHT = pl.CostEstimate(flops=1, bytes_accessed=1, transcendentals=0)
ATTEND_COST = pl.CostEstimate(flops=23 * 10**9, bytes_accessed=1, transcendentals=0)
FFN_COST = pl.CostEstimate(flops=48 * 10**9, bytes_accessed=1, transcendentals=0)


def params():
    return pltpu.CompilerParams(
        dimension_semantics=("arbitrary",), vmem_limit_bytes=VMEM_CAP
    )


def attend(off, span, lohi, vec, q, seg_row, seg_col, kv):
    inner, rows = q.shape
    return pl.pallas_call(
        partial(forward_kernel, off, len(kv)),
        grid=(rows // BLK,),
        in_specs=[SMEM_SPEC, whole_block(vec.shape), col_block(inner), ROW_SEGS, whole_block(seg_col.shape)]
        + [whole_block(p.shape) for p in kv],
        out_specs=[col_block(inner), col_block(inner), col_block(8), col_block(32)],
        out_shape=[
            jax.ShapeDtypeStruct((inner, rows), BF16),
            jax.ShapeDtypeStruct((inner, rows), F32),
            jax.ShapeDtypeStruct((8, rows), F32),
            jax.ShapeDtypeStruct((32, rows), BF16),
        ],
        scratch_shapes=[TILES, pltpu.VMEM((2 * inner, span), BF16)],
        cost_estimate=ATTEND_COST,
        name="attend",
        compiler_params=params(),
    )(lohi, vec, q, seg_row, seg_col, *kv)


def attend_queries(off, span, lohi, vec, q, do, lse, delta, seg_row, seg_col, kv):
    inner, rows = q.shape
    return pl.pallas_call(
        partial(query_kernel, off, len(kv)),
        grid=(rows // BLK,),
        in_specs=[
            SMEM_SPEC,
            whole_block(vec.shape),
            col_block(inner),
            col_block(inner),
            col_block(8),
            col_block(8),
            ROW_SEGS,
            whole_block(seg_col.shape),
        ]
        + [whole_block(p.shape) for p in kv],
        out_specs=[
            col_block(inner),
            whole_block((HEADS, 8, SPAN)),
            whole_block((HEADS, 2, 8, BLK)),
        ],
        out_shape=[
            jax.ShapeDtypeStruct((inner, rows), BF16),
            jax.ShapeDtypeStruct((HEADS, 8, SPAN), F32),
            jax.ShapeDtypeStruct((HEADS, 2, 8, BLK), F32),
        ],
        scratch_shapes=[TILES, TILES, pltpu.VMEM((2 * inner, span), BF16)],
        cost_estimate=ATTEND_COST,
        name="attend_queries",
        compiler_params=params(),
    )(lohi, vec, q, do, lse, delta, seg_row, seg_col, *kv)


def attend_keys(off, span, lohi, vec, k, v, seg_row, seg_col, queries, answers):
    inner, rows = k.shape
    both = list(queries) + list(answers)
    return pl.pallas_call(
        partial(key_kernel, off, len(queries)),
        grid=(rows // BLK,),
        in_specs=[
            SMEM_SPEC,
            whole_block(vec.shape),
            col_block(inner),
            col_block(inner),
            whole_block(seg_row.shape),
            COL_SEGS,
        ]
        + [whole_block(p.shape) for p in both],
        out_specs=[col_block(inner), col_block(inner)],
        out_shape=[jax.ShapeDtypeStruct((inner, rows), BF16)] * 2,
        scratch_shapes=[
            TILES,
            pltpu.VMEM((queries[0].shape[0], span), BF16),
            pltpu.VMEM((answers[0].shape[0], span), BF16),
        ],
        cost_estimate=ATTEND_COST,
        name="attend_keys",
        compiler_params=params(),
    )(lohi, vec, k, v, seg_row, seg_col, *both)


def ffn_kernel(count, groups, order, na, nb, ca, cb, *rest):
    pieces = rest[:count]
    outs, grads = rest[count : count + 4], rest[count + 4 : count + 4 + len(groups)]
    weights, x, ct, hid, ggr, gur, sem = rest[count + 4 + len(groups) :]
    i = pl.program_id(0)
    t = na.shape[1]

    @pl.when(i == 0)
    def _():
        copies = []
        for piece in pieces:
            rows = piece.shape[2]
            for n in range(piece.shape[0]):
                k = len(copies) // 3
                at = pl.multiple_of(order[k], 16)
                for m in range(3):
                    copies.append(
                        pltpu.make_async_copy(
                            piece.at[n, m], weights.at[m, pl.ds(at, rows), :], sem.at[k, m]
                        )
                    )
        for copy in copies:
            copy.start()
        x[...] = na[...].T
        ct[...] = ca[...].T
        for copy in copies:
            copy.wait()

    @pl.when(i == 1)
    def _():
        x[...] = nb[...].T
        ct[...] = cb[...].T

    @pl.when(i < 2)
    def _():
        rows = pl.ds(pl.multiple_of(i * t, t), t)
        g = nn(x[...], weights[0])
        square = g * g
        th = jnp.tanh(GELU_K * g * (1.0 + GELU_A * square))
        part = 0.5 * (1.0 + th)
        gelu = g * part
        slope = part + 0.5 * g * (1.0 - th * th) * (GELU_K * (1.0 + 3.0 * GELU_A * square))
        u = nn(x[...], weights[1])
        h = (gelu * u).astype(BF16)
        gh = nn(ct[...], weights[2])
        gg = (gh * u * slope).astype(BF16)
        gu = (gh * gelu).astype(BF16)
        hid[rows, :] = h
        ggr[rows, :] = gg
        gur[rows, :] = gu
        out = nt(weights[2], h).astype(BF16)
        gn = (nt(weights[0], gg) + nt(weights[1], gu)).astype(BF16)

        @pl.when(i == 0)
        def _():
            outs[0][...] = out
            outs[2][...] = gn

        @pl.when(i == 1)
        def _():
            outs[1][...] = out
            outs[3][...] = gn

    @pl.when(i >= 2)
    def _():
        blocks, tile = grads[0].shape[0], grads[0].shape[2]
        size = blocks * tile
        rows = pl.ds(pl.multiple_of((i - 2) * size, 16), size)

        def product(first, second, right):
            return (nn(first[rows, :], right[:t, :]) + nn(second[rows, :], right[t:, :])).astype(BF16)

        lefts = ((na, nb, ggr), (na, nb, gur), (ca, cb, hid))
        for g, members in enumerate(groups):
            for n, m in enumerate(members):
                value = product(*lefts[m])
                for b in range(blocks):
                    grads[g][b, n] = value[b * tile : (b + 1) * tile]


def ffn(n_own, n_other, c_own, c_other, pieces, starts, groups):
    depth, t = n_own.shape
    cols = pieces[0].shape[3]
    tile = depth // 4
    scalars = jnp.stack([jnp.asarray(v, jnp.int32) for v in starts])
    whole = pl.BlockSpec((depth, t), lambda i, o: (0, 0), pipeline_mode=pl.Buffered(1))
    result = pl.BlockSpec((depth, t), lambda i, o: (0, 0))
    place = pl.BlockSpec(memory_space=pl.ANY)
    grads = [
        pl.BlockSpec((2, len(m), tile, cols), lambda i, o: (jnp.maximum(i - 2, 0), 0, 0, 0)) for m in groups
    ]
    return pl.pallas_call(
        partial(ffn_kernel, len(pieces), groups),
        grid_spec=pltpu.PrefetchScalarGridSpec(
            num_scalar_prefetch=1,
            grid=(4,),
            in_specs=[whole] * 4 + [place] * len(pieces),
            out_specs=[result] * 4 + grads,
            scratch_shapes=[
                pltpu.VMEM((3, depth, cols), BF16),
                pltpu.VMEM((t, depth), BF16),
                pltpu.VMEM((t, depth), BF16),
                pltpu.VMEM((2 * t, cols), BF16),
                pltpu.VMEM((2 * t, cols), BF16),
                pltpu.VMEM((2 * t, cols), BF16),
                pltpu.SemaphoreType.DMA((len(starts), 3)),
            ],
        ),
        out_shape=[jax.ShapeDtypeStruct((depth, t), BF16)] * 4
        + [jax.ShapeDtypeStruct((4, len(m), tile, cols), BF16) for m in groups],
        cost_estimate=FFN_COST,
        name="ffn",
        compiler_params=params(),
    )(scalars, n_own, n_other, c_own, c_other, *pieces)


def projection_kernel(rows, core, normed, branch, dq, dk, dv, att, extra, send, keep, left, right, value):
    t, cols = normed.shape[1], dq.shape[0]

    @pl.when(pl.program_id(0) == 0)
    def _():
        left[:, :t] = normed[...]
        left[:, t:] = branch[...]
        right[...] = jnp.zeros_like(right)

    for n, part in enumerate((dq, dk, dv)):
        right[n * cols : (n + 1) * cols, :t] = part[...]
    right[3 * cols :, t:] = att[...]
    value[...] = nt(left[...], right[...])
    for p in range(send.shape[0]):
        for ref, c in ((keep, core[0]), (send, 1 - core[0])):
            r = 2 * p + c
            block = value[pl.ds(pl.multiple_of(r * rows, 8), rows), :]
            ref[p, 0] = jnp.concatenate([block, extra[r]], axis=0).astype(BF16)


def project(core, normed, branch, dq, dk, dv, att, extra, n_seq):
    depth, t = normed.shape
    cols = dq.shape[0] // n_seq
    n_dp, more, wide = extra.shape
    rows = depth // n_dp
    whole = pl.BlockSpec((depth, t), lambda z: (0, 0))
    part = pl.BlockSpec((cols, t), lambda z: (z, 0))
    shape = (n_dp // 2, n_seq, rows + more, wide)
    result = pl.BlockSpec((n_dp // 2, 1) + shape[2:], lambda z: (0, z, 0, 0))
    return pl.pallas_call(
        partial(projection_kernel, rows),
        grid=(n_seq,),
        in_specs=[
            SMEM_SPEC,
            whole,
            whole,
            part,
            part,
            part,
            part,
            pl.BlockSpec(extra.shape, lambda z: (0, 0, 0)),
        ],
        out_specs=[result, result],
        out_shape=[jax.ShapeDtypeStruct(shape, BF16)] * 2,
        scratch_shapes=[
            pltpu.VMEM((depth, 2 * t), BF16),
            pltpu.VMEM((wide, 2 * t), BF16),
            pltpu.VMEM((depth, wide), F32),
        ],
        cost_estimate=pl.CostEstimate(flops=10**10, bytes_accessed=1, transcendentals=0),
        name="project",
        compiler_params=params(),
    )(core, normed, branch, dq, dk, dv, att, extra)


def rms_scale(x):
    return lax.rsqrt(jnp.mean(x * x, axis=0, keepdims=True) + EPS)


def norm_back(grad, x, scale, gain):
    gain_grad = jnp.sum(grad * (x * scale), axis=1)
    weighted = grad * gain
    dots = jnp.mean(weighted * x, axis=0, keepdims=True)
    return scale * weighted - x * (scale * scale * scale * dots), gain_grad


def on_device(
    n_dp,
    n_seq,
    inputs,
    segments,
    cotangent,
    w_query,
    w_key,
    w_value,
    w_out,
    w_gate,
    w_up,
    w_down,
    gain_attn,
    gain_ffn,
    rel_table,
):
    mv = Moves(n_dp, n_seq)
    seqs, rows, depth = inputs.shape
    source = inputs.reshape(seqs * rows, depth).T.astype(F32)
    tangent = cotangent.reshape(seqs * rows, depth).T
    rw, sc = w_query.shape
    inner = sc * n_seq
    wide_cols = 4 * sc
    seg_rows = -(-rows // wide_cols)
    rp = -(-(rw + 2 + seg_rows) // 16) * 16

    body = jnp.concatenate([w_query, w_key, w_value, w_out.T], axis=1)
    table_row = rel_table.reshape(-1)
    pad_to = lambda v: jnp.pad(v, (0, -v.shape[0] % wide_cols)).reshape(-1, wide_cols)
    packed = jnp.concatenate(
        [
            body,
            pad_to(jnp.concatenate([gain_attn, gain_ffn])),
            pad_to(table_row),
            pad_to(segments.reshape(rows).astype(BF16)),
            jnp.zeros((rp - rw - 2 - seg_rows, wide_cols), BF16),
        ],
        axis=0,
    )
    att, stages = gather_small(mv, packed)
    full = att[:, :, :rw, :].reshape(n_seq, depth, wide_cols)
    gain_one = att[0, :, rw, :rw].reshape(depth, 1).astype(F32)
    gain_two = att[0, :, rw, rw : 2 * rw].reshape(depth, 1).astype(F32)
    table = att[0, :, rw + 1, : table_row.shape[0]].reshape(BUCKETS, HEADS)
    here = lax.dynamic_index_in_dim(att, lax.axis_index("dp"), 1, keepdims=False)
    seg_seq = here[:, rw + 2 : rw + 2 + seg_rows, :].reshape(n_seq, -1)[:, :rows].astype(jnp.int32)

    scale_one = rms_scale(source)
    normed = ((source * scale_one) * gain_one).astype(BF16)
    qkv = jnp.einsum("zdc,dt->zct", full[:, :, : 3 * sc], normed, preferred_element_type=F32)
    qkv = jnp.transpose(qkv.astype(BF16).reshape(n_seq, 3, sc, rows), (1, 0, 2, 3))
    q = qkv[0].reshape(inner, rows)
    k = qkv[1].reshape(inner, rows)
    v = qkv[2].reshape(inner, rows)

    zh = n_seq // 2
    small = small_plane(mv)
    tangent_other = mv.rotate(tangent, "c")
    cores = gather_core(mv, jnp.stack([w_gate, w_up, w_down.T]), (q, tangent_other))
    kv_halo = halo(mv, after(jnp.concatenate([k, v], 0), cores[0]))
    pieces, starts = [], []
    for j in range(zh):
        full_block = lax.all_gather(cores[j], "dp", axis_index_groups=mv.same_core())
        if small:
            pieces.append([full_block])
            starts.append([jnp.int32(2 * rw * k) for k in range(4)])
        else:
            pieces.append([jnp.moveaxis(full_block, 0, 1).reshape(1, 3, depth, -1)])
            starts.append([jnp.int32(0)])

    off = -(-MAX_DOC // BLK) * BLK
    span = 2 * off + rows
    blocks = span // BLK
    seg_own = segments.reshape(rows)
    line = jnp.pad(seg_seq.reshape(-1), (off, off), constant_values=-1)
    seg_all = lax.dynamic_slice_in_dim(line, mv.index["z"] * rows, span, 0)
    seg_row = seg_all.reshape(blocks, 1, BLK)
    seg_col = seg_all.reshape(span, 1)
    own_row = seg_own.reshape(rows // BLK, 1, BLK)
    own_col = seg_own.reshape(rows, 1)
    spots = jnp.arange(span, dtype=jnp.int32)
    firsts = seg_own[::BLK]
    lasts = seg_own[BLK - 1 :: BLK]
    low = jnp.min(jnp.where(seg_all[None] == firsts[:, None], spots[None], 1 << 20), axis=1) // BLK
    high = jnp.max(jnp.where(seg_all[None] == lasts[:, None], spots[None], -1), axis=1) // BLK + 1
    lohi = jnp.stack([low, high], 1).astype(jnp.int32)

    buckets = bucket_table()
    buckets = np.concatenate([buckets[-1:], buckets[:0:-1]])
    chosen = jnp.asarray((buckets[:, None] == np.arange(BUCKETS)[None, :]), BF16)
    vec = dot(table, chosen, ((0,), (1,)))

    attended, exact, lse, lse_parts = attend(
        off, span, lohi, vec, q, own_row, seg_col, kv_halo
    )
    q_halo = halo(mv, jnp.concatenate([q, lse_parts], 0))

    mixed = source + jnp.einsum(
        "zdc,zct->dt", full[:, :, 3 * sc :], attended.reshape(n_seq, sc, rows), preferred_element_type=F32
    )
    scale_two = rms_scale(mixed)
    normed_two = ((mixed * scale_two) * gain_two).astype(BF16)

    normed_other = mv.rotate(normed_two, "c")
    parts, sums = [], []
    for j in range(zh):
        results = ffn(
            after(normed_two, *(list(parts[-1]) + q_halo if j else ())),
            normed_other,
            tangent,
            tangent_other,
            pieces[j],
            starts[j],
            ((0, 1, 2),) if j + 1 < zh else ((0, 1), (2,)),
        )
        parts.append(results[:4])
        sums.append([ZSum(mv, j, scatter_plane(mv, grad)) for grad in results[4:]])
    out_own, out_other, gn_own, gn_other = (
        sum(four[m].astype(F32) for four in parts) for m in range(4)
    )
    gn_recv = mv.rotate(gn_other.astype(BF16), "c")
    grad_n2 = gn_own + gn_recv.astype(F32)

    grad_mixed, grad_gain_two = norm_back(grad_n2, mixed, scale_two, gain_two)
    grad_mixed = grad_mixed + tangent.astype(F32)
    grad_branch = grad_mixed.astype(BF16)
    grad_att = jnp.einsum(
        "zdc,dt->zct", full[:, :, 3 * sc :], grad_branch, preferred_element_type=F32
    )
    grad_att = grad_att.reshape(inner, rows).astype(BF16)
    delta = jnp.sum((grad_att.astype(F32) * exact).reshape(HEADS, inner // HEADS, rows), axis=1)
    delta = jnp.pad(delta, ((0, 8 - HEADS), (0, 0)))
    delta_top = lax.reduce_precision(delta, 8, 7)
    answers = jnp.concatenate([grad_att, delta_top.astype(BF16), (delta - delta_top).astype(BF16)], 0)
    do_halo = halo(mv, answers, False)

    dq, near, far = attend_queries(
        off, span, lohi, vec, q, grad_att, lse, delta, own_row, seg_col, kv_halo
    )
    out_recv = mv.rotate(after(out_other.astype(BF16), do_halo[0]), "c")
    outputs = (mixed + out_own + out_recv.astype(F32)).astype(BF16)
    swaps = [u.swap(do_halo[0]) for u in sums[0]]
    k_then = after(k, dq, *swaps)
    dk, dv = attend_keys(off, span, lohi, vec, k_then, v, seg_row, own_col, q_halo, do_halo)
    if small:
        dk = after(dk, *[u.inwards() for u in sums[0]])

    sheared = jnp.roll(jnp.sum(near, axis=1), BLK, axis=1)
    grad_table = jnp.dot(sheared, chosen.astype(F32), precision=lax.Precision.HIGHEST).T
    far_sums = jnp.sum(far, axis=(2, 3))
    grad_table = grad_table.at[31].add(far_sums[:, 0]).at[15].add(far_sums[:, 1])

    split = lambda x: x.reshape(n_seq, sc, rows)
    rows_z = jnp.concatenate([split(dq), split(dk), split(dv)], axis=1)
    grad_normed = jnp.einsum(
        "zdc,zct->dt", full[:, :, : 3 * sc], rows_z, preferred_element_type=F32
    )
    grad_source, grad_gain_one = norm_back(grad_normed, source, scale_one, gain_one)
    input_grad = (grad_mixed + grad_source).astype(BF16)

    gain_rows = jnp.concatenate(
        [grad_gain_one.reshape(n_dp, rw), grad_gain_two.reshape(n_dp, rw)], axis=1
    )
    widen = lambda x: jnp.pad(x, ((0, 0), (0, wide_cols - x.shape[1])))[:, None, :]
    extra = jnp.concatenate(
        [
            widen(gain_rows),
            widen(grad_table.reshape(n_dp, -1)),
            jnp.zeros((n_dp, rp - rw - 2, wide_cols), F32),
        ],
        axis=1,
    )
    core = mv.index["c"]
    if small and rw % 8 == 0 and rp % 16 == 0:
        send, keep = project(
            core.reshape(1).astype(jnp.int32), normed, grad_branch, dq, dk, dv, attended, extra, n_seq
        )
    else:
        g_in = jnp.einsum("dt,zct->zdc", normed, rows_z, preferred_element_type=F32)
        g_out = jnp.einsum("dt,zct->zdc", grad_branch, split(attended), preferred_element_type=F32)
        grads = jnp.concatenate([g_in, g_out], axis=2).reshape(n_seq, n_dp, rw, wide_cols)
        below = jnp.broadcast_to(extra[None], (n_seq,) + extra.shape)
        grads = jnp.concatenate([grads, below], axis=2).astype(BF16)
        grads = grads.reshape(n_seq, n_dp // 2, 2, rp, wide_cols)
        take = lambda c: jnp.moveaxis(lax.dynamic_index_in_dim(grads, c, 2, keepdims=False), 1, 0)
        send, keep = take(1 - core), take(core)
    if small:
        (first,), (wide, thin) = sums
        send = after(send, first.across())
        wide.swap(send)
    else:
        for units in sums[1:]:
            for u in units:
                u.swap(None)

    own, both = scatter_small(mv, send, keep)
    if small:
        thin.swap(both)
        first.home()
        for step in (ZSum.inwards, ZSum.across, ZSum.home):
            step(wide)
            step(thin)
    own_ffn = z_totals(mv, sums)

    return (
        outputs.T.reshape(seqs, rows, depth),
        input_grad.T.reshape(seqs, rows, depth),
        own[:rw, :sc],
        own[:rw, sc : 2 * sc],
        own[:rw, 2 * sc : 3 * sc],
        own[:rw, 3 * sc :].T,
        own_ffn[0],
        own_ffn[1],
        own_ffn[2].T,
        own[rw, :rw],
        own[rw, rw : 2 * rw],
        own[rw + 1, : table_row.shape[0]].reshape(rel_table.shape),
    )


def solution(mesh):
    row, col = P("dp", "seq"), P("seq", "dp")
    tokens = P("dp", "seq", None)
    return jax.shard_map(
        partial(on_device, mesh.shape["dp"], mesh.shape["seq"]),
        mesh=mesh,
        in_specs=(tokens, row, tokens, row, row, row, col, row, row, col, P("dp"), P("dp"), P("dp", None)),
        out_specs=(tokens, tokens, row, row, row, col, row, row, col, P("dp"), P("dp"), P("dp", None)),
        check_vma=False,
    )
```

profile of v0, /device:TPU:10, one launch (start us, length us, event | category | flops | bytes accessed | tf_op | source)
XLA Modules:
  0.0 582.9 jit_solution(7733559872030208856)
XLA Ops:
  23.2 5.7 collective-permute-done.2
  42.6 7.8 %collective-permute-done.4 = bf16[2,2,192,384]{3,2,0,1:T(8,128)(2,1)S(1)} collective-permute-done((bf16[2,2,192,384]{3,2,0,1:T(8,128)(2,1)S(1)}, bf16[2,2,192,384]{3,2,0,1:T(8,128)(2,1)S(1)}, u32[]{:S(2)}, u32[]{:S(2)}) %collective-permute-start.4) | collective-permute-done | bytes 589856 | tf_op jit(solution)/shard_map/ppermute | solution.py:66
  64.9 4.9 fusion.22
  70.8 36.2 %all-gather.9.cloned.1.call-done = bf16[12,184,896]{2,1,0:T(8,128)(2,1)} async-done(((bf16[3,184,896]{2,1,0:T(8,128)(2,1)}), bf16[12,184,896]{2,1,0:T(8,128)(2,1)}) %all-gather.9.cloned.1.call-update) | async-done | bytes 3956752 | tf_op jit(solution)/shard_map/all_gather | solution.py:134
  120.4 4.9 collective-permute-start.9
  128.9 13.7 %collective-permute-done.9.rest_3_ = bf16[768,512]{1,0:T(8,128)(2,1)S(1)} collective-permute-done((bf16[768,512]{1,0:T(8,128)(2,1)S(1)}, bf16[768,512]{1,0:T(8,128)(2,1)S(1)}, u32[]{:S(2)}, u32[]{:S(2)}) %collective-permute-start.9) | collective-permute-done | bytes 786464 | tf_op jit(solution)/shard_map/ppermute | solution.py:69
  148.0 6.5 %collective-permute-start.10 = (bf16[768,384]{1,0:T(8,128)(2,1)S(1)}, bf16[768,384]{1,0:T(8,128)(2,1)}, u32[]{:S(2)}, u32[]{:S(2)}) collective-permute-start(bf16[768,384]{1,0:T(8,128)(2,1)S(1)} %get-tuple-element.131), channel_id=1, source_target_pairs={{0,2},{1,3},{4,6},{5,7},{8,10},{9,11},{12,14},{13,15},{16,18},{17,... | collective-permute-start | bytes 1769480 | tf_op jit(solution)/shard_map/ppermute | solution.py:69
  159.1 4.7 collective-permute-done.11.rest_4_
  163.9 12.8 %collective-permute-done.10.rest_0_ = bf16[768,384]{1,0:T(8,128)(2,1)} collective-permute-done((bf16[768,384]{1,0:T(8,128)(2,1)S(1)}, bf16[768,384]{1,0:T(8,128)(2,1)}, u32[]{:S(2)}, u32[]{:S(2)}) %collective-permute-start.10) | collective-permute-done | bytes 589856 | tf_op jit(solution)/shard_map/ppermute | solution.py:69
  176.6 24.5 %attend.1 = (bf16[384,512]{1,0:T(8,128)(2,1)}, f32[384,512]{1,0:T(8,128)}, f32[8,512]{1,0:T(8,128)}, bf16[32,512]{1,0:T(8,128)(2,1)}) custom-call(s32[2,2]{1,0:T(2,128)} %pad_add_fusion.lohi, f32[6,1024]{1,0:T(8,128)} %fusion.65.vec, bf16[384,512]{1,0:T(8,128)(2,1)} %bitcast.225, s32[2,1,256]{2,1,0:T(1,128)} %bitcast.241, s32[2560,1]{1,0:T(8,128)} %reshape.371.segk, ...), custom_call_target="tpu_custom_call" | custom-call | flops 23000000512 | bytes 1 | tf_op jit(solution)/shard_map/attend/pallas_call | solution.py:478
  209.2 43.8 %ffn.2 = (bf16[1472,512]{1,0:T(8,128)(2,1)}, bf16[1472,512]{1,0:T(8,128)(2,1)}, bf16[1472,512]{1,0:T(8,128)(2,1)}, bf16[1472,512]{1,0:T(8,128)(2,1)}, bf16[4,3,368,896]{3,2,1,0:T(8,128)(2,1)}) custom-call(s32[4]{0:T(128)} %iota_multiply_fusion.order, bf16[1472,512]{1,0:T(8,128)(2,1)} %copy-done.21, bf16[1472,512]{1,0:T(8,128)(2,1)} %collective-permute-done.12.nb, ...), custom_call_target="tpu_custom_call" | custom-call | flops 48000000000 | bytes 1 | tf_op jit(solution)/shard_map/ffn/pallas_call | solution.py:649
  259.9 7.9 %collective-permute-done.16.rest_3_ = bf16[416,512]{1,0:T(8,128)(2,1)S(1)} collective-permute-done((bf16[416,512]{1,0:T(8,128)(2,1)S(1)}, bf16[416,512]{1,0:T(8,128)(2,1)S(1)}, u32[]{:S(2)}, u32[]{:S(2)}) %collective-permute-start.16) | collective-permute-done | bytes 426016 | tf_op jit(solution)/shard_map/ppermute | solution.py:69
  271.2 5.5 collective-permute-start.17
  276.7 4.8 collective-permute-done.18.rest_4_
  281.5 7.0 %collective-permute-done.17.rest_0_ = bf16[416,384]{1,0:T(8,128)(2,1)S(1)} collective-permute-done((bf16[416,384]{1,0:T(8,128)(2,1)S(1)}, bf16[416,384]{1,0:T(8,128)(2,1)S(1)}, u32[]{:S(2)}, u32[]{:S(2)}) %collective-permute-start.17) | collective-permute-done | bytes 319520 | tf_op jit(solution)/shard_map/ppermute | solution.py:69
  289.3 42.9 %ffn.3 = (bf16[1472,512]{1,0:T(8,128)(2,1)}, bf16[1472,512]{1,0:T(8,128)(2,1)}, bf16[1472,512]{1,0:T(8,128)(2,1)}, bf16[1472,512]{1,0:T(8,128)(2,1)}, bf16[4,2,3...) custom-call(s32[4]{0:T(128)} %iota_multiply_fusion.order, bf16[1472,512]{1,0:T(8,128)(2,1)} %copy-done.21, ...), custom_call_target="tpu_custom_call" | custom-call | flops 48000000000 | bytes 1 | tf_op jit(solution)/shard_map/ffn/pallas_call | solution.py:649
  351.3 5.8 %collective-permute-start.20 = (bf16[400,384]{1,0:T(8,128)(2,1)}, bf16[400,384]{1,0:T(8,128)(2,1)}, u32[]{:S(2)}, u32[]{:S(2)}) collective-permute-start(bf16[400,384]{1,0:T(8,128)(2,1)} %get-tuple-element.139), channel_id=1, source_target_pairs={{0,2},{1,3},{4,6},{5,7},{8,10},{9,11},{12,14},{13,15},{16,18},{17,... | collective-permute-start | bytes 921608 | tf_op jit(solution)/shard_map/ppermute | solution.py:69
  368.0 6.1 %reduce-scatter.16.cloned.1.call-done = bf16[1,3,368,896]{3,2,1,0:T(8,128)(2,1)} async-done(((bf16[4,3,368,896]{3,2,1,0:T(8,128)(2,1)}), bf16[1,3,368,896]{3,2,1,0:T(8,128)(2,1)}) %reduce-scatter.16.cloned.1.call-update) | async-done | bytes 1978384
  376.3 24.6 %attend_queries.1 = (bf16[384,512]{1,0:T(8,128)(2,1)}, f32[6,8,1024]{2,1,0:T(8,128)}, f32[6,2,8,256]{3,2,1,0:T(8,128)}) custom-call(s32[2,2]{1,0:T(2,128)} %pad_add_fusion.lohi, f32[6,1024]{1,0:T(8,128)} %fusion.65.vec, bf16[384,512]{1,0:T(8,128)(2,1)} %bitcast.226, bf16[384,512]{1,0:T(8,128)(2,1)} %bitcast.216, f32[8,512]{1,0:T(8,128)} %get-tuple-element.85.lse, ...), custom_call_target="tpu_custom_call" | custom-call | flops 23000000512 | bytes 1 | tf_op jit(solution)/shard_map/attend_queries/pallas_call | solution.py:499
  409.4 4.6 collective-permute-done.25.rest_9_
  413.9 23.2 %attend_keys.1 = (bf16[384,512]{1,0:T(8,128)(2,1)}, bf16[384,512]{1,0:T(8,128)(2,1)}) custom-call(s32[2,2]{1,0:T(2,128)} %pad_add_fusion.lohi, f32[6,1024]{1,0:T(8,128)} %fusion.65.vec, bf16[384,512]{1,0:T(8,128)(2,1)} %bitcast.222, bf16[384,512]{1,0:T(8,128)(2,1)} %bitcast.224, s32[10,1,256]{2,1,0:T(1,128)} %reshape.349.segq, s32[512,1]{1,0:T(8,128)} %copy.104.segk, ...), custom_call_target="tpu_custom_call" | custom-call | flops 23000000512 | bytes 1 | tf_op jit(solution)/shard_map/attend_keys/pallas_call | solution.py:533
  437.1 6.9 %fusion.15 = (f32[1472]{0:T(1024)S(1)}, f32[512]{0:T(512)S(1)}, f32[1472,512]{1,0:T(8,128)}) fusion(bf16[1,512,1472]{1,2,0:T(8,128)(2,1)S(1)} %copy-done.3, f32[512]{0:T(512)S(1)} %copy-done.35, f32[1472]{0:T(1024)S(1)} %copy-done.31, bf16[4,96,512]{2,1,0:T(8,128)(2,1)} %bitcast.253, bf16[4,96,512]{2,1,0:T(8,128)(2,1)} %bitcast.252, ...), kind=kOutput, calls=%fused_computation.19 | convolution fusion | flops 1745254400 | bytes 10239488 | tf_op jit(solution)/shard_map/zdc,zct->dt/dot_general | solution.py:895
  446.0 9.7 %collective-permute-start.27 = (bf16[3,184,896]{2,1,0:T(8,128)(2,1)S(1)}, bf16[3,184,896]{2,1,0:T(8,128)(2,1)S(1)}, u32[]{:S(2)}, u32[]{:S(2)}) collective-permute-start(bf16[3,184,896]{2,1,0:T(8,128)(2,1)S(1)} %add_convert_fusion.5), channel_id=1, source_target_pairs={{1,2},{2,1},{5,6},{6,5},{9,10},{10,9},{13,14},{14,13},{17,18},{18,... | collective-permute-start | bytes 2967560 | tf_op jit(solution)/shard_map/ppermute | solution.py:69
  456.4 11.1 %project.1 = (bf16[4,4,192,384]{3,2,1,0:T(8,128)(2,1)}, bf16[4,4,192,384]{3,2,1,0:T(8,128)(2,1)}) custom-call(s32[1]{0:T(128)} %bitcast.63.core, bf16[1472,512]{1,0:T(8,128)(2,1)} %copy-done.20, bf16[1472,512]{1,0:T(8,128)(2,1)} %copy-done.5, bf16[384,512]{1,0:T(8,128)(2,1)} %get-tuple-element.86.dq, bf16[384,512]{1,0:T(8,128)(2,1)} %get-tuple-element.91.dk, ...), custom_call_target="tpu_custom_call" | custom-call | flops 10000000000 | bytes 1 | tf_op jit(solution)/shard_map/project/pallas_call | solution.py:703
  467.5 8.6 %collective-permute-done.27 = bf16[3,184,896]{2,1,0:T(8,128)(2,1)S(1)} collective-permute-done((bf16[3,184,896]{2,1,0:T(8,128)(2,1)S(1)}, bf16[3,184,896]{2,1,0:T(8,128)(2,1)S(1)}, u32[]{:S(2)}, u32[]{:S(2)}) %collective-permute-start.27) | collective-permute-done | bytes 989216 | tf_op jit(solution)/shard_map/ppermute | solution.py:69
  476.1 4.7 collective-permute-done.28
  497.4 4.5 fusion.25
  503.5 11.2 %collective-permute-done.31 = bf16[2,184,896]{2,1,0:T(8,128)(2,1)} collective-permute-done((bf16[2,184,896]{2,1,0:T(8,128)(2,1)}, bf16[2,184,896]{2,1,0:T(8,128)(2,1)}, u32[]{:S(2)}, u32[]{:S(2)}) %collective-permute-start.31) | collective-permute-done | bytes 659488 | tf_op jit(solution)/shard_map/ppermute | solution.py:69
  527.8 8.0 %collective-permute-done.32 = bf16[2,184,896]{2,1,0:T(8,128)(2,1)S(1)} collective-permute-done((bf16[2,184,896]{2,1,0:T(8,128)(2,1)S(1)}, bf16[2,184,896]{2,1,0:T(8,128)(2,1)S(1)}, u32[]{:S(2)}, u32[]{:S(2)}) %collective-permute-start.32) | collective-permute-done | bytes 659488 | tf_op jit(solution)/shard_map/ppermute | solution.py:69
  542.5 4.6 fusion.26
  547.1 14.5 %collective-permute-done.33 = bf16[2,184,896]{2,1,0:T(8,128)(2,1)} collective-permute-done((bf16[2,184,896]{2,1,0:T(8,128)(2,1)S(1)}, bf16[2,184,896]{2,1,0:T(8,128)(2,1)}, u32[]{:S(2)}, u32[]{:S(2)}) %collective-permute-start.33) | collective-permute-done | bytes 659488 | tf_op jit(solution)/shard_map/ppermute | solution.py:69
  562.9 5.9 %collective-permute-done.37 = bf16[1,184,896]{2,1,0:T(8,128)(2,1)} collective-permute-done((bf16[1,184,896]{2,1,0:T(8,128)(2,1)S(1)}, bf16[1,184,896]{2,1,0:T(8,128)(2,1)}, u32[]{:S(2)}, u32[]{:S(2)}) %collective-permute-start.37) | collective-permute-done | bytes 329760 | tf_op jit(solution)/shard_map/ppermute | solution.py:69
  (292 shorter events, 180.0 us)
Async XLA Ops:
  7.2 99.8 %all-gather.9.cloned.1.call-start = ((), (), s32[]{:S(2)}) async-start(), calls=%async_computation.8 | async-start | bytes 4945920 | tf_op jit(solution)/shard_map/all_gather | solution.py:134
  30.9 178.3 %all-gather.5.cloned.1.call-start = ((), (), s32[]{:S(2)}) async-start(), calls=%async_computation.5 | async-start | bytes 9891840 | tf_op jit(solution)/shard_map/all_gather | solution.py:803
  36.1 14.3 %collective-permute-start.4 = (bf16[2,2,192,384]{3,2,0,1:T(8,128)(2,1)S(1)}, bf16[2,2,192,384]{3,2,0,1:T(8,128)(2,1)S(1)}, u32[]{:S(2)}, u32[]{:S(2)}) collective-permute-start(bf16[2,2,192,384]{3,2,0,1:T(8,128)(2,1)S(1)} %pad_maximum_fusion.5), channel_id=1, source_target_pairs={{0,16},{4,20},{8,24},{12,28},{16,0},{20,4},{24,8},{28,12},{1,17},{... | collective-permute-start | bytes 1769480 | tf_op jit(solution)/shard_map/ppermute | solution.py:66
  52.8 57.2 %collective-permute-start.13 = (bf16[1472,512]{1,0:T(8,128)(2,1)}, bf16[1472,512]{1,0:T(8,128)(2,1)}, u32[]{:S(2)}, u32[]{:S(2)}) collective-permute-start(bf16[1472,512]{1,0:T(8,128)(2,1)} %bitcast.37.ca), channel_id=1, source_target_pairs={{0,4},{4,0},{8,12},{12,8},{16,20},{20,16},{24,28},{28,24},{1,5},{5... | collective-permute-start | bytes 4521992 | tf_op jit(solution)/shard_map/ppermute | solution.py:66
  118.0 171.3 %all-gather.7.cloned.1.call-start = ((), (), s32[]{:S(2)}) async-start(), calls=%async_computation.6 | async-start | bytes 9891840 | tf_op jit(solution)/shard_map/all_gather | solution.py:803
  119.5 254.6 %reduce-scatter.16.cloned.1.call-start = ((), (), s32[]{:S(2)}) async-start(), calls=%async_computation.9 | async-start | bytes 9891840
  120.4 22.2 %collective-permute-start.9 = (bf16[768,512]{1,0:T(8,128)(2,1)S(1)}, bf16[768,512]{1,0:T(8,128)(2,1)S(1)}, u32[]{:S(2)}, u32[]{:S(2)}) collective-permute-start(bf16[768,512]{1,0:T(8,128)(2,1)S(1)} %pad_maximum_fusion.4.rest_2_), channel_id=1, source_target_pairs={{1,0},{2,1},{3,2},{5,4},{6,5},{7,6},{9,8},{10,9},{11,10},{13,12},{... | collective-permute-start | bytes 2359304 | tf_op jit(solution)/shard_map/ppermute | solution.py:69
  125.3 21.3 %collective-permute-start.8 = (bf16[768,512]{1,0:T(8,128)(2,1)S(1)}, bf16[768,512]{1,0:T(8,128)(2,1)}, u32[]{:S(2)}, u32[]{:S(2)}) collective-permute-start(bf16[768,512]{1,0:T(8,128)(2,1)S(1)} %pad_maximum_fusion.4.rest_2_), channel_id=1, source_target_pairs={{0,1},{1,2},{2,3},{4,5},{5,6},{6,7},{8,9},{9,10},{10,11},{12,13},{... | collective-permute-start | bytes 2359304 | tf_op jit(solution)/shard_map/ppermute | solution.py:69
  146.7 17.1 %collective-permute-start.11 = (bf16[768,384]{1,0:T(8,128)(2,1)S(1)}, bf16[768,384]{1,0:T(8,128)(2,1)S(1)}, u32[]{:S(2)}, u32[]{:S(2)}) collective-permute-start(bf16[768,384]{1,0:T(8,128)(2,1)S(1)} %get-tuple-element.130), channel_id=1, source_target_pairs={{2,0},{3,1},{6,4},{7,5},{10,8},{11,9},{14,12},{15,13},{18,16},{19,... | collective-permute-start | bytes 1769480 | tf_op jit(solution)/shard_map/ppermute | solution.py:69
  148.0 28.6 %collective-permute-start.10 = (bf16[768,384]{1,0:T(8,128)(2,1)S(1)}, bf16[768,384]{1,0:T(8,128)(2,1)}, u32[]{:S(2)}, u32[]{:S(2)}) collective-permute-start(bf16[768,384]{1,0:T(8,128)(2,1)S(1)} %get-tuple-element.131), channel_id=1, source_target_pairs={{0,2},{1,3},{4,6},{5,7},{8,10},{9,11},{12,14},{13,15},{16,18},{17,... | collective-permute-start | bytes 1769480 | tf_op jit(solution)/shard_map/ppermute | solution.py:69
  253.1 235.1 %reduce-scatter.20.cloned.1.call-start = ((), (), s32[]{:S(2)}) async-start(), calls=%async_computation.11 | async-start | bytes 6594560
  254.1 13.7 %collective-permute-start.16 = (bf16[416,512]{1,0:T(8,128)(2,1)S(1)}, bf16[416,512]{1,0:T(8,128)(2,1)S(1)}, u32[]{:S(2)}, u32[]{:S(2)}) collective-permute-start(bf16[416,512]{1,0:T(8,128)(2,1)S(1)} %pad_maximum_fusion.7.rest_2_), channel_id=1, source_target_pairs={{1,0},{2,1},{3,2},{5,4},{6,5},{7,6},{9,8},{10,9},{11,10},{13,12},{... | collective-permute-start | bytes 1277960 | tf_op jit(solution)/shard_map/ppermute | solution.py:69
  256.0 13.8 %collective-permute-start.15 = (bf16[416,512]{1,0:T(8,128)(2,1)S(1)}, bf16[416,512]{1,0:T(8,128)(2,1)}, u32[]{:S(2)}, u32[]{:S(2)}) collective-permute-start(bf16[416,512]{1,0:T(8,128)(2,1)S(1)} %pad_maximum_fusion.7.rest_2_), channel_id=1, source_target_pairs={{0,1},{1,2},{2,3},{4,5},{5,6},{6,7},{8,9},{9,10},{10,11},{12,13},{... | collective-permute-start | bytes 1277960 | tf_op jit(solution)/shard_map/ppermute | solution.py:69
  269.9 11.6 %collective-permute-start.18 = (bf16[416,384]{1,0:T(8,128)(2,1)S(1)}, bf16[416,384]{1,0:T(8,128)(2,1)S(1)}, u32[]{:S(2)}, u32[]{:S(2)}) collective-permute-start(bf16[416,384]{1,0:T(8,128)(2,1)S(1)} %get-tuple-element.136), channel_id=1, source_target_pairs={{2,0},{3,1},{6,4},{7,5},{10,8},{11,9},{14,12},{15,13},{18,16},{19,... | collective-permute-start | bytes 958472 | tf_op jit(solution)/shard_map/ppermute | solution.py:69
  271.2 17.3 %collective-permute-start.17 = (bf16[416,384]{1,0:T(8,128)(2,1)S(1)}, bf16[416,384]{1,0:T(8,128)(2,1)S(1)}, u32[]{:S(2)}, u32[]{:S(2)}) collective-permute-start(bf16[416,384]{1,0:T(8,128)(2,1)S(1)} %get-tuple-element.137), channel_id=1, source_target_pairs={{0,2},{1,3},{4,6},{5,7},{8,10},{9,11},{12,14},{13,15},{16,18},{17,... | collective-permute-start | bytes 958472 | tf_op jit(solution)/shard_map/ppermute | solution.py:69
  332.2 164.0 %reduce-scatter.22.cloned.1.call-start = ((), (), s32[]{:S(2)}) async-start(), calls=%async_computation.12 | async-start | bytes 3297280
  351.3 16.7 %collective-permute-start.20 = (bf16[400,384]{1,0:T(8,128)(2,1)}, bf16[400,384]{1,0:T(8,128)(2,1)}, u32[]{:S(2)}, u32[]{:S(2)}) collective-permute-start(bf16[400,384]{1,0:T(8,128)(2,1)} %get-tuple-element.139), channel_id=1, source_target_pairs={{0,2},{1,3},{4,6},{5,7},{8,10},{9,11},{12,14},{13,15},{16,18},{17,... | collective-permute-start | bytes 921608 | tf_op jit(solution)/shard_map/ppermute | solution.py:69
  358.7 183.8 %reduce-scatter.18.cloned.1.call-start = ((), (), s32[]{:S(2)}) async-start(), calls=%async_computation.10 | async-start | bytes 2949120
  358.8 55.2 %collective-permute-start.24 = (bf16[400,512]{1,0:T(8,128)(2,1)S(1)}, bf16[400,512]{1,0:T(8,128)(2,1)}, u32[]{:S(2)}, u32[]{:S(2)}) collective-permute-start(bf16[400,512]{1,0:T(8,128)(2,1)S(1)} %copy-done.16), channel_id=1, source_target_pairs={{1,0},{2,1},{3,2},{5,4},{6,5},{7,6},{9,8},{10,9},{11,10},{13,12},{... | collective-permute-start | bytes 1228808 | tf_op jit(solution)/shard_map/ppermute | solution.py:69
  360.7 53.3 %collective-permute-start.23 = (bf16[400,512]{1,0:T(8,128)(2,1)S(1)}, bf16[400,512]{1,0:T(8,128)(2,1)}, u32[]{:S(2)}, u32[]{:S(2)}) collective-permute-start(bf16[400,512]{1,0:T(8,128)(2,1)S(1)} %copy-done.16), channel_id=1, source_target_pairs={{0,1},{1,2},{2,3},{4,5},{5,6},{6,7},{8,9},{9,10},{10,11},{12,13},{... | collective-permute-start | bytes 1228808 | tf_op jit(solution)/shard_map/ppermute | solution.py:69
  376.3 29.8 %collective-permute-start.22 = (bf16[3,184,896]{2,1,0:T(8,128)(2,1)}, bf16[3,184,896]{2,1,0:T(8,128)(2,1)}, u32[]{:S(2)}, u32[]{:S(2)}) collective-permute-start(bf16[3,184,896]{2,1,0:T(8,128)(2,1)} %dynamic-slice_bitcast_fusion), channel_id=1, source_target_pairs={{0,4},{4,0},{8,12},{12,8},{16,20},{20,16},{24,28},{28,24},{1,5},{5... | collective-permute-start | bytes 2967560 | tf_op jit(solution)/shard_map/ppermute | solution.py:66
  402.9 11.0 %collective-permute-start.25 = (bf16[400,384]{1,0:T(8,128)(2,1)}, bf16[400,384]{1,0:T(8,128)(2,1)}, u32[]{:S(2)}, u32[]{:S(2)}) collective-permute-start(bf16[400,384]{1,0:T(8,128)(2,1)} %get-tuple-element.138), channel_id=1, source_target_pairs={{2,0},{3,1},{6,4},{7,5},{10,8},{11,9},{14,12},{15,13},{18,16},{19,... | collective-permute-start | bytes 921608 | tf_op jit(solution)/shard_map/ppermute | solution.py:69
  407.8 29.3 %collective-permute-start.26 = (bf16[3,184,896]{2,1,0:T(8,128)(2,1)S(1)}, bf16[3,184,896]{2,1,0:T(8,128)(2,1)}, u32[]{:S(2)}, u32[]{:S(2)}) collective-permute-start(bf16[3,184,896]{2,1,0:T(8,128)(2,1)S(1)} %bitcast_select_fusion.1), channel_id=1, source_target_pairs={{0,1},{3,2},{4,5},{7,6},{8,9},{11,10},{12,13},{15,14},{16,17},{19,... | collective-permute-start | bytes 2967560 | tf_op jit(solution)/shard_map/ppermute | solution.py:69
  446.0 30.1 %collective-permute-start.27 = (bf16[3,184,896]{2,1,0:T(8,128)(2,1)S(1)}, bf16[3,184,896]{2,1,0:T(8,128)(2,1)S(1)}, u32[]{:S(2)}, u32[]{:S(2)}) collective-permute-start(bf16[3,184,896]{2,1,0:T(8,128)(2,1)S(1)} %add_convert_fusion.5), channel_id=1, source_target_pairs={{1,2},{2,1},{5,6},{6,5},{9,10},{10,9},{13,14},{14,13},{17,18},{18,... | collective-permute-start | bytes 2967560 | tf_op jit(solution)/shard_map/ppermute | solution.py:69
  484.6 88.1 %reduce-scatter.14.cloned.1.call-start = ((), (), s32[]{:S(2)}) async-start(), calls=%async_computation.7 | async-start | bytes 737280 | tf_op jit(solution)/shard_map/reduce_scatter | solution.py:219
  494.9 19.9 %collective-permute-start.31 = (bf16[2,184,896]{2,1,0:T(8,128)(2,1)}, bf16[2,184,896]{2,1,0:T(8,128)(2,1)}, u32[]{:S(2)}, u32[]{:S(2)}) collective-permute-start(bf16[2,184,896]{2,1,0:T(8,128)(2,1)} %bitcast_select_fusion.2), channel_id=1, source_target_pairs={{0,1},{3,2},{4,5},{7,6},{8,9},{11,10},{12,13},{15,14},{16,17},{19,... | collective-permute-start | bytes 1978376 | tf_op jit(solution)/shard_map/ppermute | solution.py:69
  501.9 18.9 %collective-permute-start.35 = (bf16[1,184,896]{2,1,0:T(8,128)(2,1)S(1)}, bf16[1,184,896]{2,1,0:T(8,128)(2,1)S(1)}, u32[]{:S(2)}, u32[]{:S(2)}) collective-permute-start(bf16[1,184,896]{2,1,0:T(8,128)(2,1)S(1)} %bitcast_select_fusion.4), channel_id=1, source_target_pairs={{0,1},{3,2},{4,5},{7,6},{8,9},{11,10},{12,13},{15,14},{16,17},{19,... | collective-permute-start | bytes 989192 | tf_op jit(solution)/shard_map/ppermute | solution.py:69
  516.2 19.7 %collective-permute-start.32 = (bf16[2,184,896]{2,1,0:T(8,128)(2,1)S(1)}, bf16[2,184,896]{2,1,0:T(8,128)(2,1)S(1)}, u32[]{:S(2)}, u32[]{:S(2)}) collective-permute-start(bf16[2,184,896]{2,1,0:T(8,128)(2,1)S(1)} %add_convert_fusion.7), channel_id=1, source_target_pairs={{1,2},{2,1},{5,6},{6,5},{9,10},{10,9},{13,14},{14,13},{17,18},{18,... | collective-permute-start | bytes 1978376 | tf_op jit(solution)/shard_map/ppermute | solution.py:69
  521.0 20.1 %collective-permute-start.36 = (bf16[1,184,896]{2,1,0:T(8,128)(2,1)S(1)}, bf16[1,184,896]{2,1,0:T(8,128)(2,1)S(1)}, u32[]{:S(2)}, u32[]{:S(2)}) collective-permute-start(bf16[1,184,896]{2,1,0:T(8,128)(2,1)S(1)} %add_convert_fusion.9), channel_id=1, source_target_pairs={{1,2},{2,1},{5,6},{6,5},{9,10},{10,9},{13,14},{14,13},{17,18},{18,... | collective-permute-start | bytes 989192 | tf_op jit(solution)/shard_map/ppermute | solution.py:69
  525.4 44.4 %collective-permute-start.29 = (bf16[3,184,896]{2,1,0:T(8,128)(2,1)S(1)}, bf16[3,184,896]{2,1,0:T(8,128)(2,1)}, u32[]{:S(2)}, u32[]{:S(2)}) collective-permute-start(bf16[3,184,896]{2,1,0:T(8,128)(2,1)S(1)} %add_convert_fusion.4), channel_id=1, source_target_pairs={{1,0},{3,2},{5,4},{7,6},{9,8},{11,10},{13,12},{15,14},{17,16},{19,... | collective-permute-start | bytes 2967560 | tf_op jit(solution)/shard_map/ppermute | solution.py:69
  536.1 25.6 %collective-permute-start.33 = (bf16[2,184,896]{2,1,0:T(8,128)(2,1)S(1)}, bf16[2,184,896]{2,1,0:T(8,128)(2,1)}, u32[]{:S(2)}, u32[]{:S(2)}) collective-permute-start(bf16[2,184,896]{2,1,0:T(8,128)(2,1)S(1)} %add_convert_fusion.6), channel_id=1, source_target_pairs={{0,1},{2,3},{4,5},{6,7},{8,9},{10,11},{12,13},{14,15},{16,17},{18,... | collective-permute-start | bytes 1978376 | tf_op jit(solution)/shard_map/ppermute | solution.py:69
  541.2 27.6 %collective-permute-start.37 = (bf16[1,184,896]{2,1,0:T(8,128)(2,1)S(1)}, bf16[1,184,896]{2,1,0:T(8,128)(2,1)}, u32[]{:S(2)}, u32[]{:S(2)}) collective-permute-start(bf16[1,184,896]{2,1,0:T(8,128)(2,1)S(1)} %add_convert_fusion.8), channel_id=1, source_target_pairs={{0,1},{2,3},{4,5},{6,7},{8,9},{10,11},{12,13},{14,15},{16,17},{18,... | collective-permute-start | bytes 989192 | tf_op jit(solution)/shard_map/ppermute | solution.py:69
  (59 other events, 731.9 us)
Sparse Core Ops, SparseCore 0:
  31.0 75.9 all-gather.8
  118.1 84.5 all-gather.4
  204.6 83.6 all-gather.6
  291.3 82.7 reduce-scatter.15
  377.2 61.7 reduce-scatter.19
  442.1 40.4 reduce-scatter.21
  485.7 37.4 reduce-scatter.17
  542.6 24.5 reduce-scatter.13
where the time goes:
time: 590 us; the launch traced here: 583 us
  waiting for transfers between devices  208 us (35%)
  Pallas kernels  170 us (29%)
  starting transfers between devices  78 us (13%)
  other arithmetic  56.9 us (10%)
  local copies, waits for them, and re-layouts  34.4 us (6%)
  matrix products  20.3 us (3%)
  between operations  15.4 us (3%)
    ppermute x21, waiting for transfers between devices, zperm(): return lax.ppermute(x, 'seq', pairs)  117 us
    pallas_call x2, Pallas kernels, ffn(): pl.pallas_call(partial(ffn_kernel, len(pieces), groups), grid_spec=pltpu....  86.7 us
    ppermute x21, starting transfers between devices, zperm(): return lax.ppermute(x, 'seq', pairs)  66.6 us
    all_gather x1, waiting for transfers between devices, gather_core(): full = lax.all_gather(w, 'seq')  36.2 us
    ppermute x14, waiting for transfers between devices, rotate(): return lax.ppermute(x, 'dp', pairs)  35.3 us
    pallas_call x1, Pallas kernels, attend_queries(): pl.pallas_call(partial(query_kernel, off, len(kv)), grid=(rows // BLK,),...  24.6 us
    pallas_call x1, Pallas kernels, attend(): pl.pallas_call(partial(forward_kernel, off, len(kv)), grid=(rows // BLK,)...  24.5 us
    pallas_call x1, Pallas kernels, attend_keys(): pl.pallas_call(partial(key_kernel, off, len(queries)), grid=(rows // BLK,...  23.2 us
  transfers between devices with their start and end apart: 46, of which 32 were waited for; matrix products, arithmetic and copies ran while one was open for 16% of the time, Pallas kernels for 29%

commit v1 on v0

--- a/solution.py
+++ b/solution.py
@@ -880,10 +880,10 @@
     out_recv = mv.rotate(after(out_other.astype(BF16), do_halo[0]), "c")
     outputs = (mixed + out_own + out_recv.astype(F32)).astype(BF16)
     swaps = [u.swap(do_halo[0]) for u in sums[0]]
-    k_then = after(k, dq, *swaps)
+    k_then = after(k, dq)
     dk, dv = attend_keys(off, span, lohi, vec, k_then, v, seg_row, own_col, q_halo, do_halo)
     if small:
-        dk = after(dk, *[u.inwards() for u in sums[0]])
+        dk = after(dk, *swaps)
 
     sheared = jnp.roll(jnp.sum(near, axis=1), BLK, axis=1)
     grad_table = jnp.dot(sheared, chosen.astype(F32), precision=lax.Precision.HIGHEST).T
@@ -926,7 +926,7 @@
         send, keep = take(1 - core), take(core)
     if small:
         (first,), (wide, thin) = sums
-        send = after(send, first.across())
+        send = after(send, first.inwards())
         wide.swap(send)
     else:
         for units in sums[1:]:
@@ -936,6 +936,7 @@
     own, both = scatter_small(mv, send, keep)
     if small:
         thin.swap(both)
+        first.across()
         first.home()
         for step in (ZSum.inwards, ZSum.across, ZSum.home):
             step(wide)

time: 590 us -> 587 us (level)
  waiting for transfers between devices: 208 us -> 198 us
  other arithmetic: 56.9 us -> 64 us
  starting transfers between devices: 78 us -> 71 us
    ppermute x21, starting transfers between devices: 66.6 us -> 59.8 us  [zperm(): return lax.ppermute(x, 'seq', pairs)]
    unnamed x12, waiting for transfers between devices: 6.24 us -> 0.18 us
  transfers between devices with their start and end apart: 46 -> 46, of which waited for: 32 -> 29; matrix products, arithmetic and copies ran while one was open for 16% -> 18% of each run, Pallas kernels for 29% -> 30%
where the time goes in v1:
time: 587 us; the launch traced here: 576 us
  waiting for transfers between devices  198 us (34%)
  Pallas kernels  170 us (29%)
  starting transfers between devices  71 us (12%)
  other arithmetic  64 us (11%)
  local copies, waits for them, and re-layouts  36.5 us (6%)
  matrix products  20.7 us (4%)
  between operations  15.4 us (3%)
    ppermute x21, waiting for transfers between devices, zperm(): return lax.ppermute(x, 'seq', pairs)  117 us
    pallas_call x2, Pallas kernels, ffn(): pl.pallas_call(partial(ffn_kernel, len(pieces), groups), grid_spec=pltpu....  86.7 us
    ppermute x21, starting transfers between devices, zperm(): return lax.ppermute(x, 'seq', pairs)  59.8 us
    all_gather x1, waiting for transfers between devices, gather_core(): full = lax.all_gather(w, 'seq')  36.2 us
    ppermute x14, waiting for transfers between devices, rotate(): return lax.ppermute(x, 'dp', pairs)  31.5 us
    pallas_call x1, Pallas kernels, attend_queries(): pl.pallas_call(partial(query_kernel, off, len(kv)), grid=(rows // BLK,),...  24.6 us
    pallas_call x1, Pallas kernels, attend(): pl.pallas_call(partial(forward_kernel, off, len(kv)), grid=(rows // BLK,)...  24.5 us
    pallas_call x1, Pallas kernels, attend_keys(): pl.pallas_call(partial(key_kernel, off, len(queries)), grid=(rows // BLK,...  23.3 us
  transfers between devices with their start and end apart: 46, of which 29 were waited for; matrix products, arithmetic and copies ran while one was open for 18% of the time, Pallas kernels for 30%

profile of v1, /device:TPU:10, one launch (start us, length us, event | category | flops | bytes accessed | tf_op | source)
XLA Modules:
  0.0 576.1 jit_solution(14848808925412751614)
XLA Ops:
  23.2 5.7 collective-permute-done.2
  42.6 7.8 %collective-permute-done.4 = bf16[2,2,192,384]{3,2,0,1:T(8,128)(2,1)S(1)} collective-permute-done((bf16[2,2,192,384]{3,2,0,1:T(8,128)(2,1)S(1)}, bf16[2,2,192,384]{3,2,0,1:T(8,128)(2,1)S(1)}, u32[]{:S(2)}, u32[]{:S(2)}) %collective-permute-start.4) | collective-permute-done | bytes 589856 | tf_op jit(solution)/shard_map/ppermute | solution.py:66
  64.9 4.9 fusion.22
  70.8 36.2 %all-gather.9.cloned.1.call-done = bf16[12,184,896]{2,1,0:T(8,128)(2,1)} async-done(((bf16[3,184,896]{2,1,0:T(8,128)(2,1)}), bf16[12,184,896]{2,1,0:T(8,128)(2,1)}) %all-gather.9.cloned.1.call-update) | async-done | bytes 3956752 | tf_op jit(solution)/shard_map/all_gather | solution.py:134
  120.4 4.9 collective-permute-start.9
  128.9 13.7 %collective-permute-done.9.rest_3_ = bf16[768,512]{1,0:T(8,128)(2,1)S(1)} collective-permute-done((bf16[768,512]{1,0:T(8,128)(2,1)S(1)}, bf16[768,512]{1,0:T(8,128)(2,1)S(1)}, u32[]{:S(2)}, u32[]{:S(2)}) %collective-permute-start.9) | collective-permute-done | bytes 786464 | tf_op jit(solution)/shard_map/ppermute | solution.py:69
  148.0 6.5 %collective-permute-start.10 = (bf16[768,384]{1,0:T(8,128)(2,1)S(1)}, bf16[768,384]{1,0:T(8,128)(2,1)}, u32[]{:S(2)}, u32[]{:S(2)}) collective-permute-start(bf16[768,384]{1,0:T(8,128)(2,1)S(1)} %get-tuple-element.131), channel_id=1, source_target_pairs={{0,2},{1,3},{4,6},{5,7},{8,10},{9,11},{12,14},{13,15},{16,18},{17,... | collective-permute-start | bytes 1769480 | tf_op jit(solution)/shard_map/ppermute | solution.py:69
  159.1 4.7 collective-permute-done.11.rest_4_
  163.9 12.8 %collective-permute-done.10.rest_0_ = bf16[768,384]{1,0:T(8,128)(2,1)} collective-permute-done((bf16[768,384]{1,0:T(8,128)(2,1)S(1)}, bf16[768,384]{1,0:T(8,128)(2,1)}, u32[]{:S(2)}, u32[]{:S(2)}) %collective-permute-start.10) | collective-permute-done | bytes 589856 | tf_op jit(solution)/shard_map/ppermute | solution.py:69
  176.6 24.5 %attend.1 = (bf16[384,512]{1,0:T(8,128)(2,1)}, f32[384,512]{1,0:T(8,128)}, f32[8,512]{1,0:T(8,128)}, bf16[32,512]{1,0:T(8,128)(2,1)}) custom-call(s32[2,2]{1,0:T(2,128)} %pad_add_fusion.lohi, f32[6,1024]{1,0:T(8,128)} %fusion.65.vec, bf16[384,512]{1,0:T(8,128)(2,1)} %bitcast.225, s32[2,1,256]{2,1,0:T(1,128)} %bitcast.241, s32[2560,1]{1,0:T(8,128)} %reshape.371.segk, ...), custom_call_target="tpu_custom_call" | custom-call | flops 23000000512 | bytes 1 | tf_op jit(solution)/shard_map/attend/pallas_call | solution.py:478
  209.2 43.8 %ffn.2 = (bf16[1472,512]{1,0:T(8,128)(2,1)}, bf16[1472,512]{1,0:T(8,128)(2,1)}, bf16[1472,512]{1,0:T(8,128)(2,1)}, bf16[1472,512]{1,0:T(8,128)(2,1)}, bf16[4,3,368,896]{3,2,1,0:T(8,128)(2,1)}) custom-call(s32[4]{0:T(128)} %iota_multiply_fusion.order, bf16[1472,512]{1,0:T(8,128)(2,1)} %copy-done.22, bf16[1472,512]{1,0:T(8,128)(2,1)} %collective-permute-done.12.nb, ...), custom_call_target="tpu_custom_call" | custom-call | flops 48000000000 | bytes 1 | tf_op jit(solution)/shard_map/ffn/pallas_call | solution.py:649
  259.9 7.9 %collective-permute-done.16.rest_3_ = bf16[416,512]{1,0:T(8,128)(2,1)S(1)} collective-permute-done((bf16[416,512]{1,0:T(8,128)(2,1)S(1)}, bf16[416,512]{1,0:T(8,128)(2,1)S(1)}, u32[]{:S(2)}, u32[]{:S(2)}) %collective-permute-start.16) | collective-permute-done | bytes 426016 | tf_op jit(solution)/shard_map/ppermute | solution.py:69
  271.2 5.5 collective-permute-start.17
  276.7 4.8 collective-permute-done.18.rest_4_
  281.5 7.0 %collective-permute-done.17.rest_0_ = bf16[416,384]{1,0:T(8,128)(2,1)S(1)} collective-permute-done((bf16[416,384]{1,0:T(8,128)(2,1)S(1)}, bf16[416,384]{1,0:T(8,128)(2,1)S(1)}, u32[]{:S(2)}, u32[]{:S(2)}) %collective-permute-start.17) | collective-permute-done | bytes 319520 | tf_op jit(solution)/shard_map/ppermute | solution.py:69
  289.3 42.9 %ffn.3 = (bf16[1472,512]{1,0:T(8,128)(2,1)}, bf16[1472,512]{1,0:T(8,128)(2,1)}, bf16[1472,512]{1,0:T(8,128)(2,1)}, bf16[1472,512]{1,0:T(8,128)(2,1)}, bf16[4,2,3...) custom-call(s32[4]{0:T(128)} %iota_multiply_fusion.order, bf16[1472,512]{1,0:T(8,128)(2,1)} %copy-done.22, ...), custom_call_target="tpu_custom_call" | custom-call | flops 48000000000 | bytes 1 | tf_op jit(solution)/shard_map/ffn/pallas_call | solution.py:649
  343.4 4.6 fusion.58
  363.8 24.6 %attend_queries.1 = (bf16[384,512]{1,0:T(8,128)(2,1)}, f32[6,8,1024]{2,1,0:T(8,128)}, f32[6,2,8,256]{3,2,1,0:T(8,128)}) custom-call(s32[2,2]{1,0:T(2,128)} %pad_add_fusion.lohi, f32[6,1024]{1,0:T(8,128)} %fusion.65.vec, bf16[384,512]{1,0:T(8,128)(2,1)} %bitcast.226, bf16[384,512]{1,0:T(8,128)(2,1)} %bitcast.216, f32[8,512]{1,0:T(8,128)} %get-tuple-element.85.lse, ...), custom_call_target="tpu_custom_call" | custom-call | flops 23000000512 | bytes 1 | tf_op jit(solution)/shard_map/attend_queries/pallas_call | solution.py:499
  391.6 6.9 %collective-permute-start.20 = (bf16[400,384]{1,0:T(8,128)(2,1)}, bf16[400,384]{1,0:T(8,128)(2,1)}, u32[]{:S(2)}, u32[]{:S(2)}) collective-permute-start(bf16[400,384]{1,0:T(8,128)(2,1)} %get-tuple-element.139), channel_id=1, source_target_pairs={{0,2},{1,3},{4,6},{5,7},{8,10},{9,11},{12,14},{13,15},{16,18},{17,... | collective-permute-start | bytes 921608 | tf_op jit(solution)/shard_map/ppermute | solution.py:69
  400.2 8.5 %collective-permute-done.20.rest_5_ = bf16[400,384]{1,0:T(8,128)(2,1)} collective-permute-done((bf16[400,384]{1,0:T(8,128)(2,1)}, bf16[400,384]{1,0:T(8,128)(2,1)}, u32[]{:S(2)}, u32[]{:S(2)}) %collective-permute-start.20) | collective-permute-done | bytes 307232 | tf_op jit(solution)/shard_map/ppermute | solution.py:69
  411.0 23.3 %attend_keys.1 = (bf16[384,512]{1,0:T(8,128)(2,1)}, bf16[384,512]{1,0:T(8,128)(2,1)}) custom-call(s32[2,2]{1,0:T(2,128)} %pad_add_fusion.lohi, f32[6,1024]{1,0:T(8,128)} %fusion.65.vec, bf16[384,512]{1,0:T(8,128)(2,1)} %bitcast.222, bf16[384,512]{1,0:T(8,128)(2,1)} %bitcast.224, s32[10,1,256]{2,1,0:T(1,128)} %reshape.349.segq, s32[512,1]{1,0:T(8,128)} %copy.104.segk, ...), custom_call_target="tpu_custom_call" | custom-call | flops 23000000512 | bytes 1 | tf_op jit(solution)/shard_map/attend_keys/pallas_call | solution.py:533
  434.4 7.2 %fusion.15 = (f32[1472]{0:T(1024)S(1)}, f32[512]{0:T(512)S(1)}, f32[1472,512]{1,0:T(8,128)}) fusion(bf16[1,512,1472]{1,2,0:T(8,128)(2,1)S(1)} %copy-done.3, f32[512]{0:T(512)S(1)} %copy-done.37, f32[1472]{0:T(1024)S(1)} %copy-done.33, bf16[4,96,512]{2,1,0:T(8,128)(2,1)} %bitcast.253, bf16[4,96,512]{2,1,0:T(8,128)(2,1)} %bitcast.252, ...), kind=kOutput, calls=%fused_computation.19 | convolution fusion | flops 1745254400 | bytes 10239488 | tf_op jit(solution)/shard_map/zdc,zct->dt/dot_general | solution.py:895
  445.4 11.1 %project.1 = (bf16[4,4,192,384]{3,2,1,0:T(8,128)(2,1)}, bf16[4,4,192,384]{3,2,1,0:T(8,128)(2,1)}) custom-call(s32[1]{0:T(128)} %bitcast.62.core, bf16[1472,512]{1,0:T(8,128)(2,1)} %copy-done.21, bf16[1472,512]{1,0:T(8,128)(2,1)} %copy-done.5, bf16[384,512]{1,0:T(8,128)(2,1)} %get-tuple-element.86.dq, bf16[384,512]{1,0:T(8,128)(2,1)} %get-tuple-element.91.dk, ...), custom_call_target="tpu_custom_call" | custom-call | flops 10000000000 | bytes 1 | tf_op jit(solution)/shard_map/project/pallas_call | solution.py:703
  456.5 10.6 %collective-permute-done.26 = bf16[3,184,896]{2,1,0:T(8,128)(2,1)S(1)} collective-permute-done((bf16[3,184,896]{2,1,0:T(8,128)(2,1)S(1)}, bf16[3,184,896]{2,1,0:T(8,128)(2,1)S(1)}, u32[]{:S(2)}, u32[]{:S(2)}) %collective-permute-start.26) | collective-permute-done | bytes 989216 | tf_op jit(solution)/shard_map/ppermute | solution.py:69
  467.1 4.7 collective-permute-done.27
  491.1 4.7 fusion.25
  497.4 11.2 %collective-permute-done.31 = bf16[2,184,896]{2,1,0:T(8,128)(2,1)} collective-permute-done((bf16[2,184,896]{2,1,0:T(8,128)(2,1)}, bf16[2,184,896]{2,1,0:T(8,128)(2,1)}, u32[]{:S(2)}, u32[]{:S(2)}) %collective-permute-start.31) | collective-permute-done | bytes 659488 | tf_op jit(solution)/shard_map/ppermute | solution.py:69
  513.7 4.9 collective-permute-start.36
  522.6 7.2 %collective-permute-done.32 = bf16[2,184,896]{2,1,0:T(8,128)(2,1)S(1)} collective-permute-done((bf16[2,184,896]{2,1,0:T(8,128)(2,1)S(1)}, bf16[2,184,896]{2,1,0:T(8,128)(2,1)S(1)}, u32[]{:S(2)}, u32[]{:S(2)}) %collective-permute-start.32) | collective-permute-done | bytes 659488 | tf_op jit(solution)/shard_map/ppermute | solution.py:69
  536.4 4.6 fusion.26
  540.9 10.5 %collective-permute-done.33 = bf16[2,184,896]{2,1,0:T(8,128)(2,1)} collective-permute-done((bf16[2,184,896]{2,1,0:T(8,128)(2,1)S(1)}, bf16[2,184,896]{2,1,0:T(8,128)(2,1)}, u32[]{:S(2)}, u32[]{:S(2)}) %collective-permute-start.33) | collective-permute-done | bytes 659488 | tf_op jit(solution)/shard_map/ppermute | solution.py:69
  552.6 9.4 %collective-permute-done.37 = bf16[1,184,896]{2,1,0:T(8,128)(2,1)} collective-permute-done((bf16[1,184,896]{2,1,0:T(8,128)(2,1)S(1)}, bf16[1,184,896]{2,1,0:T(8,128)(2,1)}, u32[]{:S(2)}, u32[]{:S(2)}) %collective-permute-start.37) | collective-permute-done | bytes 329760 | tf_op jit(solution)/shard_map/ppermute | solution.py:69
  (298 shorter events, 173.4 us)
Async XLA Ops:
  7.2 99.8 %all-gather.9.cloned.1.call-start = ((), (), s32[]{:S(2)}) async-start(), calls=%async_computation.8 | async-start | bytes 4945920 | tf_op jit(solution)/shard_map/all_gather | solution.py:134
  30.9 178.3 %all-gather.5.cloned.1.call-start = ((), (), s32[]{:S(2)}) async-start(), calls=%async_computation.5 | async-start | bytes 9891840 | tf_op jit(solution)/shard_map/all_gather | solution.py:803
  36.1 14.3 %collective-permute-start.4 = (bf16[2,2,192,384]{3,2,0,1:T(8,128)(2,1)S(1)}, bf16[2,2,192,384]{3,2,0,1:T(8,128)(2,1)S(1)}, u32[]{:S(2)}, u32[]{:S(2)}) collective-permute-start(bf16[2,2,192,384]{3,2,0,1:T(8,128)(2,1)S(1)} %pad_maximum_fusion.5), channel_id=1, source_target_pairs={{0,16},{4,20},{8,24},{12,28},{16,0},{20,4},{24,8},{28,12},{1,17},{... | collective-permute-start | bytes 1769480 | tf_op jit(solution)/shard_map/ppermute | solution.py:66
  52.8 57.2 %collective-permute-start.13 = (bf16[1472,512]{1,0:T(8,128)(2,1)}, bf16[1472,512]{1,0:T(8,128)(2,1)}, u32[]{:S(2)}, u32[]{:S(2)}) collective-permute-start(bf16[1472,512]{1,0:T(8,128)(2,1)} %bitcast.37.ca), channel_id=1, source_target_pairs={{0,4},{4,0},{8,12},{12,8},{16,20},{20,16},{24,28},{28,24},{1,5},{5... | collective-permute-start | bytes 4521992 | tf_op jit(solution)/shard_map/ppermute | solution.py:66
  118.0 171.3 %all-gather.7.cloned.1.call-start = ((), (), s32[]{:S(2)}) async-start(), calls=%async_computation.6 | async-start | bytes 9891840 | tf_op jit(solution)/shard_map/all_gather | solution.py:803
  119.5 289.2 %reduce-scatter.16.cloned.1.call-start = ((), (), s32[]{:S(2)}) async-start(), calls=%async_computation.9 | async-start | bytes 9891840
  120.4 22.2 %collective-permute-start.9 = (bf16[768,512]{1,0:T(8,128)(2,1)S(1)}, bf16[768,512]{1,0:T(8,128)(2,1)S(1)}, u32[]{:S(2)}, u32[]{:S(2)}) collective-permute-start(bf16[768,512]{1,0:T(8,128)(2,1)S(1)} %pad_maximum_fusion.4.rest_2_), channel_id=1, source_target_pairs={{1,0},{2,1},{3,2},{5,4},{6,5},{7,6},{9,8},{10,9},{11,10},{13,12},{... | collective-permute-start | bytes 2359304 | tf_op jit(solution)/shard_map/ppermute | solution.py:69
  125.3 21.3 %collective-permute-start.8 = (bf16[768,512]{1,0:T(8,128)(2,1)S(1)}, bf16[768,512]{1,0:T(8,128)(2,1)}, u32[]{:S(2)}, u32[]{:S(2)}) collective-permute-start(bf16[768,512]{1,0:T(8,128)(2,1)S(1)} %pad_maximum_fusion.4.rest_2_), channel_id=1, source_target_pairs={{0,1},{1,2},{2,3},{4,5},{5,6},{6,7},{8,9},{9,10},{10,11},{12,13},{... | collective-permute-start | bytes 2359304 | tf_op jit(solution)/shard_map/ppermute | solution.py:69
  146.7 17.1 %collective-permute-start.11 = (bf16[768,384]{1,0:T(8,128)(2,1)S(1)}, bf16[768,384]{1,0:T(8,128)(2,1)S(1)}, u32[]{:S(2)}, u32[]{:S(2)}) collective-permute-start(bf16[768,384]{1,0:T(8,128)(2,1)S(1)} %get-tuple-element.130), channel_id=1, source_target_pairs={{2,0},{3,1},{6,4},{7,5},{10,8},{11,9},{14,12},{15,13},{18,16},{19,... | collective-permute-start | bytes 1769480 | tf_op jit(solution)/shard_map/ppermute | solution.py:69
  148.0 28.6 %collective-permute-start.10 = (bf16[768,384]{1,0:T(8,128)(2,1)S(1)}, bf16[768,384]{1,0:T(8,128)(2,1)}, u32[]{:S(2)}, u32[]{:S(2)}) collective-permute-start(bf16[768,384]{1,0:T(8,128)(2,1)S(1)} %get-tuple-element.131), channel_id=1, source_target_pairs={{0,2},{1,3},{4,6},{5,7},{8,10},{9,11},{12,14},{13,15},{16,18},{17,... | collective-permute-start | bytes 1769480 | tf_op jit(solution)/shard_map/ppermute | solution.py:69
  253.1 226.4 %reduce-scatter.20.cloned.1.call-start = ((), (), s32[]{:S(2)}) async-start(), calls=%async_computation.11 | async-start | bytes 6594560
  254.1 13.7 %collective-permute-start.16 = (bf16[416,512]{1,0:T(8,128)(2,1)S(1)}, bf16[416,512]{1,0:T(8,128)(2,1)S(1)}, u32[]{:S(2)}, u32[]{:S(2)}) collective-permute-start(bf16[416,512]{1,0:T(8,128)(2,1)S(1)} %pad_maximum_fusion.7.rest_2_), channel_id=1, source_target_pairs={{1,0},{2,1},{3,2},{5,4},{6,5},{7,6},{9,8},{10,9},{11,10},{13,12},{... | collective-permute-start | bytes 1277960 | tf_op jit(solution)/shard_map/ppermute | solution.py:69
  256.0 13.8 %collective-permute-start.15 = (bf16[416,512]{1,0:T(8,128)(2,1)S(1)}, bf16[416,512]{1,0:T(8,128)(2,1)}, u32[]{:S(2)}, u32[]{:S(2)}) collective-permute-start(bf16[416,512]{1,0:T(8,128)(2,1)S(1)} %pad_maximum_fusion.7.rest_2_), channel_id=1, source_target_pairs={{0,1},{1,2},{2,3},{4,5},{5,6},{6,7},{8,9},{9,10},{10,11},{12,13},{... | collective-permute-start | bytes 1277960 | tf_op jit(solution)/shard_map/ppermute | solution.py:69
  271.2 17.3 %collective-permute-start.17 = (bf16[416,384]{1,0:T(8,128)(2,1)S(1)}, bf16[416,384]{1,0:T(8,128)(2,1)S(1)}, u32[]{:S(2)}, u32[]{:S(2)}) collective-permute-start(bf16[416,384]{1,0:T(8,128)(2,1)S(1)} %get-tuple-element.137), channel_id=1, source_target_pairs={{0,2},{1,3},{4,6},{5,7},{8,10},{9,11},{12,14},{13,15},{16,18},{17,... | collective-permute-start | bytes 958472 | tf_op jit(solution)/shard_map/ppermute | solution.py:69
  332.2 157.8 %reduce-scatter.22.cloned.1.call-start = ((), (), s32[]{:S(2)}) async-start(), calls=%async_computation.12 | async-start | bytes 3297280
  338.0 198.3 %reduce-scatter.18.cloned.1.call-start = ((), (), s32[]{:S(2)}) async-start(), calls=%async_computation.10 | async-start | bytes 2949120
  355.3 55.7 %collective-permute-start.23 = (bf16[400,512]{1,0:T(8,128)(2,1)}, bf16[400,512]{1,0:T(8,128)(2,1)}, u32[]{:S(2)}, u32[]{:S(2)}) collective-permute-start(bf16[400,512]{1,0:T(8,128)(2,1)} %pad_maximum_fusion.8.rest_7_), channel_id=1, source_target_pairs={{1,0},{2,1},{3,2},{5,4},{6,5},{7,6},{9,8},{10,9},{11,10},{13,12},{... | collective-permute-start | bytes 1228808 | tf_op jit(solution)/shard_map/ppermute | solution.py:69
  357.2 53.8 %collective-permute-start.22 = (bf16[400,512]{1,0:T(8,128)(2,1)}, bf16[400,512]{1,0:T(8,128)(2,1)}, u32[]{:S(2)}, u32[]{:S(2)}) collective-permute-start(bf16[400,512]{1,0:T(8,128)(2,1)} %pad_maximum_fusion.8.rest_7_), channel_id=1, source_target_pairs={{0,1},{1,2},{2,3},{4,5},{5,6},{6,7},{8,9},{9,10},{10,11},{12,13},{... | collective-permute-start | bytes 1228808 | tf_op jit(solution)/shard_map/ppermute | solution.py:69
  390.3 20.6 %collective-permute-start.24 = (bf16[400,384]{1,0:T(8,128)(2,1)S(1)}, bf16[400,384]{1,0:T(8,128)(2,1)}, u32[]{:S(2)}, u32[]{:S(2)}) collective-permute-start(bf16[400,384]{1,0:T(8,128)(2,1)S(1)} %copy-done.29), channel_id=1, source_target_pairs={{2,0},{3,1},{6,4},{7,5},{10,8},{11,9},{14,12},{15,13},{18,16},{19,... | collective-permute-start | bytes 921608 | tf_op jit(solution)/shard_map/ppermute | solution.py:69
  391.6 17.1 %collective-permute-start.20 = (bf16[400,384]{1,0:T(8,128)(2,1)}, bf16[400,384]{1,0:T(8,128)(2,1)}, u32[]{:S(2)}, u32[]{:S(2)}) collective-permute-start(bf16[400,384]{1,0:T(8,128)(2,1)} %get-tuple-element.139), channel_id=1, source_target_pairs={{0,2},{1,3},{4,6},{5,7},{8,10},{9,11},{12,14},{13,15},{16,18},{17,... | collective-permute-start | bytes 921608 | tf_op jit(solution)/shard_map/ppermute | solution.py:69
  411.0 23.4 %collective-permute-start.25 = (bf16[3,184,896]{2,1,0:T(8,128)(2,1)}, bf16[3,184,896]{2,1,0:T(8,128)(2,1)S(1)}, u32[]{:S(2)}, u32[]{:S(2)}) collective-permute-start(bf16[3,184,896]{2,1,0:T(8,128)(2,1)} %dynamic-slice_bitcast_fusion), channel_id=1, source_target_pairs={{0,4},{4,0},{8,12},{12,8},{16,20},{20,16},{24,28},{28,24},{1,5},{5... | collective-permute-start | bytes 2967560 | tf_op jit(solution)/shard_map/ppermute | solution.py:66
  443.4 23.7 %collective-permute-start.26 = (bf16[3,184,896]{2,1,0:T(8,128)(2,1)S(1)}, bf16[3,184,896]{2,1,0:T(8,128)(2,1)S(1)}, u32[]{:S(2)}, u32[]{:S(2)}) collective-permute-start(bf16[3,184,896]{2,1,0:T(8,128)(2,1)S(1)} %bitcast_select_fusion.1), channel_id=1, source_target_pairs={{0,1},{3,2},{4,5},{7,6},{8,9},{11,10},{12,13},{15,14},{16,17},{19,... | collective-permute-start | bytes 2967560 | tf_op jit(solution)/shard_map/ppermute | solution.py:69
  475.9 90.1 %reduce-scatter.14.cloned.1.call-start = ((), (), s32[]{:S(2)}) async-start(), calls=%async_computation.7 | async-start | bytes 737280 | tf_op jit(solution)/shard_map/reduce_scatter | solution.py:219
  479.3 11.8 %collective-permute-start.21 = (bf16[1472,512]{1,0:T(8,128)(2,1)}, bf16[1472,512]{1,0:T(8,128)(2,1)}, u32[]{:S(2)}, u32[]{:S(2)}) collective-permute-start(bf16[1472,512]{1,0:T(8,128)(2,1)} %add_convert_fusion.3), channel_id=1, source_target_pairs={{0,4},{4,0},{8,12},{12,8},{16,20},{20,16},{24,28},{28,24},{1,5},{5... | collective-permute-start | bytes 4521992 | tf_op jit(solution)/shard_map/ppermute | solution.py:66
  484.7 33.9 %collective-permute-start.28 = (bf16[3,184,896]{2,1,0:T(8,128)(2,1)}, bf16[3,184,896]{2,1,0:T(8,128)(2,1)}, u32[]{:S(2)}, u32[]{:S(2)}) collective-permute-start(bf16[3,184,896]{2,1,0:T(8,128)(2,1)} %add_convert_fusion.5), channel_id=1, source_target_pairs={{1,2},{2,1},{5,6},{6,5},{9,10},{10,9},{13,14},{14,13},{17,18},{18,... | collective-permute-start | bytes 2967560 | tf_op jit(solution)/shard_map/ppermute | solution.py:69
  488.7 20.0 %collective-permute-start.31 = (bf16[2,184,896]{2,1,0:T(8,128)(2,1)}, bf16[2,184,896]{2,1,0:T(8,128)(2,1)}, u32[]{:S(2)}, u32[]{:S(2)}) collective-permute-start(bf16[2,184,896]{2,1,0:T(8,128)(2,1)} %bitcast_select_fusion.2), channel_id=1, source_target_pairs={{0,1},{3,2},{4,5},{7,6},{8,9},{11,10},{12,13},{15,14},{16,17},{19,... | collective-permute-start | bytes 1978376 | tf_op jit(solution)/shard_map/ppermute | solution.py:69
  495.8 17.7 %collective-permute-start.35 = (bf16[1,184,896]{2,1,0:T(8,128)(2,1)S(1)}, bf16[1,184,896]{2,1,0:T(8,128)(2,1)S(1)}, u32[]{:S(2)}, u32[]{:S(2)}) collective-permute-start(bf16[1,184,896]{2,1,0:T(8,128)(2,1)S(1)} %bitcast_select_fusion.4), channel_id=1, source_target_pairs={{0,1},{3,2},{4,5},{7,6},{8,9},{11,10},{12,13},{15,14},{16,17},{19,... | collective-permute-start | bytes 989192 | tf_op jit(solution)/shard_map/ppermute | solution.py:69
  510.1 19.7 %collective-permute-start.32 = (bf16[2,184,896]{2,1,0:T(8,128)(2,1)S(1)}, bf16[2,184,896]{2,1,0:T(8,128)(2,1)S(1)}, u32[]{:S(2)}, u32[]{:S(2)}) collective-permute-start(bf16[2,184,896]{2,1,0:T(8,128)(2,1)S(1)} %add_convert_fusion.7), channel_id=1, source_target_pairs={{1,2},{2,1},{5,6},{6,5},{9,10},{10,9},{13,14},{14,13},{17,18},{18,... | collective-permute-start | bytes 1978376 | tf_op jit(solution)/shard_map/ppermute | solution.py:69
  513.7 21.2 %collective-permute-start.36 = (bf16[1,184,896]{2,1,0:T(8,128)(2,1)S(1)}, bf16[1,184,896]{2,1,0:T(8,128)(2,1)S(1)}, u32[]{:S(2)}, u32[]{:S(2)}) collective-permute-start(bf16[1,184,896]{2,1,0:T(8,128)(2,1)S(1)} %add_convert_fusion.9), channel_id=1, source_target_pairs={{1,2},{2,1},{5,6},{6,5},{9,10},{10,9},{13,14},{14,13},{17,18},{18,... | collective-permute-start | bytes 989192 | tf_op jit(solution)/shard_map/ppermute | solution.py:69
  520.2 42.9 %collective-permute-start.29 = (bf16[3,184,896]{2,1,0:T(8,128)(2,1)S(1)}, bf16[3,184,896]{2,1,0:T(8,128)(2,1)}, u32[]{:S(2)}, u32[]{:S(2)}) collective-permute-start(bf16[3,184,896]{2,1,0:T(8,128)(2,1)S(1)} %add_convert_fusion.4), channel_id=1, source_target_pairs={{1,0},{3,2},{5,4},{7,6},{9,8},{11,10},{13,12},{15,14},{17,16},{19,... | collective-permute-start | bytes 2967560 | tf_op jit(solution)/shard_map/ppermute | solution.py:69
  530.0 21.4 %collective-permute-start.33 = (bf16[2,184,896]{2,1,0:T(8,128)(2,1)S(1)}, bf16[2,184,896]{2,1,0:T(8,128)(2,1)}, u32[]{:S(2)}, u32[]{:S(2)}) collective-permute-start(bf16[2,184,896]{2,1,0:T(8,128)(2,1)S(1)} %add_convert_fusion.6), channel_id=1, source_target_pairs={{0,1},{2,3},{4,5},{6,7},{8,9},{10,11},{12,13},{14,15},{16,17},{18,... | collective-permute-start | bytes 1978376 | tf_op jit(solution)/shard_map/ppermute | solution.py:69
  535.0 27.0 %collective-permute-start.37 = (bf16[1,184,896]{2,1,0:T(8,128)(2,1)S(1)}, bf16[1,184,896]{2,1,0:T(8,128)(2,1)}, u32[]{:S(2)}, u32[]{:S(2)}) collective-permute-start(bf16[1,184,896]{2,1,0:T(8,128)(2,1)S(1)} %add_convert_fusion.8), channel_id=1, source_target_pairs={{0,1},{2,3},{4,5},{6,7},{8,9},{10,11},{12,13},{14,15},{16,17},{18,... | collective-permute-start | bytes 989192 | tf_op jit(solution)/shard_map/ppermute | solution.py:69
  (62 other events, 751.6 us)
Sparse Core Ops, SparseCore 0:
  31.0 75.9 all-gather.8
  118.1 84.5 all-gather.4
  204.6 83.6 all-gather.6
  291.3 82.7 reduce-scatter.15
  377.2 61.7 reduce-scatter.19
  442.1 40.5 reduce-scatter.21
  485.7 37.4 reduce-scatter.17
  536.5 26.6 reduce-scatter.13
